TPU v7x, 128 devices: a whole 4x4x4 slice. The times are simulated.
128 devices in a mesh: dp: 16 (over y_hi, z, core), tensor: 8 (over y_lo, x).
Axes of the slice: x: 4, y: 4 (y_hi: 2, y_lo: 2; y = y_hi * 2 + y_lo), z: 4, core: 2. Of those that a mesh axis runs over, the one named last changes fastest.
Arguments:
- block_input: bfloat16 [24576, 1024], P(('dp', 'tensor')), may hold values from -6 to 6
- out_cotangent: bfloat16 [24576, 1024], P(('dp', 'tensor')), may hold values from -6 to 6
- lengths: int32 [16], P('dp'), may hold values from 1024 to 1536, as said below
- mixer_gain: float32 [1024], replicated, may hold values from 0.5 to 1.5
- query_weight: bfloat16 [1024, 1024], P('dp', 'tensor'), may hold values from -0.1875 to 0.1875
- key_weight: bfloat16 [1024, 1024], P('dp', 'tensor'), may hold values from -0.1875 to 0.1875
- value_weight: bfloat16 [1024, 2048], P('dp', 'tensor'), may hold values from -0.1875 to 0.1875
- output_gate_weight: bfloat16 [1024, 2048], P('dp', 'tensor'), may hold values from -0.1875 to 0.1875
- decay_weight: bfloat16 [1024, 8, 2], P('dp', 'tensor'), may hold values from -0.1875 to 0.1875
- query_conv: float32 [4, 1024], P(None, 'tensor'), may hold values from -3 to 3
- key_conv: float32 [4, 1024], P(None, 'tensor'), may hold values from -3 to 3
- value_conv: float32 [4, 2048], P(None, 'tensor'), may hold values from -3 to 3
- decay_log: float32 [8], P('tensor'), may hold values from -6 to -2
- decay_bias: float32 [8], P('tensor'), may hold values from -2 to 1
- head_gain: float32 [256], replicated, may hold values from 0.5 to 1.5
- out_weight: bfloat16 [2048, 1024], P('tensor', 'dp'), may hold values from -0.25 to 0.25
- ffn_gain: float32 [1024], replicated, may hold values from 0.5 to 1.5
- ffn_gate: bfloat16 [1024, 2816], P('dp', 'tensor'), may hold values from -0.1875 to 0.1875
- ffn_up: bfloat16 [1024, 2816], P('dp', 'tensor'), may hold values from -0.1875 to 0.1875
- ffn_down: bfloat16 [2816, 1024], P('tensor', 'dp'), may hold values from -0.109375 to 0.109375
Outputs:
- block_output: bfloat16 [24576, 1024], P(('dp', 'tensor'))
- input_grad: float32 [24576, 1024], P(('dp', 'tensor'))
- mixer_gain_grad: float32 [1024], replicated
- query_weight_grad: float32 [1024, 1024], P('dp', 'tensor')
- key_weight_grad: float32 [1024, 1024], P('dp', 'tensor')
- value_weight_grad: float32 [1024, 2048], P('dp', 'tensor')
- output_gate_weight_grad: float32 [1024, 2048], P('dp', 'tensor')
- decay_weight_grad: float32 [1024, 8, 2], P('dp', 'tensor')
- query_conv_grad: float32 [4, 1024], P(None, 'tensor')
- key_conv_grad: float32 [4, 1024], P(None, 'tensor')
- value_conv_grad: float32 [4, 2048], P(None, 'tensor')
- decay_log_grad: float32 [8], P('tensor')
- decay_bias_grad: float32 [8], P('tensor')
- head_gain_grad: float32 [256], replicated
- out_weight_grad: float32 [2048, 1024], P('tensor', 'dp')
- ffn_gain_grad: float32 [1024], replicated
- ffn_gate_grad: float32 [1024, 2816], P('dp', 'tensor')
- ffn_up_grad: float32 [1024, 2816], P('dp', 'tensor')
- ffn_down_grad: float32 [2816, 1024], P('tensor', 'dp')
Inputs may be any that keep to these rules, and one draw needn't show every extreme that they name: lengths[g] is a multiple of 64; some group is full and some holds exactly 1024 rows.
All inputs are finite; a program needn't handle non-finite values.
Results may differ from a plain program's by a relative error of at most 0.025.
Values may be sent and summed in bfloat16 or wider, within the bound.
A program may use at most 128 MiB of HBM per device.

v0:
```python
import jax
import jax.numpy as jnp
from jax import lax
from jax.sharding import PartitionSpec as P

DK = 128
DV = 256
SPAN = 64


norm_eps = 1e-06
gate_eps = 1e-05


def exact_dot(left_side, right_side):
    return jnp.dot(left_side, right_side, precision=lax.Precision.HIGHEST)


def matmul(left_side, right_side):
    return jnp.dot(left_side, right_side, preferred_element_type=jnp.float32)


def contract_rows(left_side, right_side):
    return lax.dot_general(
        left_side, right_side, (((0,), (0,)), ((), ())), preferred_element_type=jnp.float32
    )


def times_transposed(left_side, right_side):
    return lax.dot_general(
        left_side, right_side, (((1,), (1,)), ((), ())), preferred_element_type=jnp.float32
    )


def rms_scale(values, scale_gain):
    return (
        values
        * lax.rsqrt(jnp.mean(values * values, axis=-1, keepdims=True) + norm_eps)
        * scale_gain
    )


def causal_conv(values, weight):
    row_count = values.shape[0]
    taps_count = weight.shape[0]
    padded = jnp.concatenate(
        [jnp.zeros((taps_count - 1, values.shape[1]), values.dtype), values], axis=0
    )
    summed = jnp.zeros_like(values)
    for offset in range(taps_count):
        summed = summed + weight[offset] * padded[offset : offset + row_count]
    return jax.nn.silu(summed)


def unit_inverse(lower_part):
    size_now = lower_part.shape[0]
    identity = jnp.eye(size_now, dtype=lower_part.dtype)
    powered = lower_part
    inverse = identity - lower_part
    degree = 2
    while degree < size_now:
        powered = exact_dot(powered, powered)
        inverse = exact_dot(inverse, identity + powered)
        degree = degree * 2
    return inverse


def block_step(memory, block_items):
    queries, keys_in, values, decays, write_rate = block_items
    cumul_decay = jnp.cumsum(decays)
    indices = jnp.arange(decays.shape[0])
    strict_mask = indices[:, None] > indices[None, :]
    causal_mask = indices[:, None] >= indices[None, :]
    spread = cumul_decay[:, None] - cumul_decay[None, :]
    strict_ratio = jnp.where(strict_mask, jnp.exp(jnp.where(strict_mask, spread, 0.0)), 0.0)
    causal_ratio = jnp.where(causal_mask, jnp.exp(jnp.where(causal_mask, spread, 0.0)), 0.0)
    lower_part = write_rate[:, None] * exact_dot(keys_in, keys_in.T) * strict_ratio
    inverse = unit_inverse(lower_part)
    growth = jnp.exp(cumul_decay)
    target = write_rate[:, None] * (values - exact_dot(growth[:, None] * keys_in, memory.T))
    fresh = exact_dot(inverse, target)
    scores = exact_dot(queries, keys_in.T) * causal_ratio
    result = exact_dot(growth[:, None] * queries, memory.T) + exact_dot(scores, fresh)
    tail_decay = jnp.exp(cumul_decay[-1] - cumul_decay)
    memory = growth[-1] * memory + exact_dot(fresh.T, tail_decay[:, None] * keys_in)
    return (memory, result)


def delta_head(queries, keys_in, values, decays, write_rate):
    row_count = decays.shape[0]
    blocks_count = row_count // SPAN

    def into_blocks(array):
        return array.reshape((blocks_count, SPAN) + array.shape[1:])

    start_memory = jnp.zeros((DV, DK), jnp.float32)
    final_memory, results = lax.scan(
        jax.checkpoint(block_step),
        start_memory,
        (
            into_blocks(queries),
            into_blocks(keys_in),
            into_blocks(values),
            into_blocks(decays),
            into_blocks(write_rate),
        ),
    )
    return results.reshape(row_count, DV)


def mixer_core(
    query_pre,
    key_pre,
    value_pre,
    gate_pre,
    decay_pre,
    query_conv,
    key_conv,
    value_conv,
    decay_log,
    decay_bias,
    head_gain,
):
    row_count = query_pre.shape[0]
    head_count = query_pre.shape[1] // DK
    queries = causal_conv(query_pre, query_conv).reshape(row_count, head_count, DK)
    keys_in = causal_conv(key_pre, key_conv).reshape(row_count, head_count, DK)
    values = causal_conv(value_pre, value_conv).reshape(row_count, head_count, DV)
    queries = (
        queries
        * lax.rsqrt(jnp.sum(queries * queries, axis=-1, keepdims=True) + norm_eps)
        * DK ** (-0.5)
    )
    keys_in = keys_in * lax.rsqrt(jnp.sum(keys_in * keys_in, axis=-1, keepdims=True) + norm_eps)
    decays = -jnp.exp(decay_log) * jax.nn.softplus(decay_pre[:, :, 0] + decay_bias)
    write_rate = jax.nn.sigmoid(decay_pre[:, :, 1])
    outputs = jax.vmap(delta_head, in_axes=1, out_axes=1)(
        queries, keys_in, values, decays, write_rate
    )
    normed = (
        outputs
        * lax.rsqrt(jnp.mean(outputs * outputs, axis=-1, keepdims=True) + gate_eps)
        * head_gain
    )
    gated = normed * jax.nn.silu(gate_pre.reshape(row_count, head_count, DV))
    return gated.reshape(row_count, head_count * DV)


def group_rows(values):
    return lax.all_gather(values, "tensor", axis=0, tiled=True)


def row_sums(values):
    return lax.psum_scatter(
        values.astype(jnp.bfloat16), "tensor", scatter_dimension=0, tiled=True
    ).astype(jnp.float32)


def shards(
    block_input,
    out_cotangent,
    lengths,
    mixer_gain,
    query_weight,
    key_weight,
    value_weight,
    output_gate_weight,
    decay_weight,
    query_conv,
    key_conv,
    value_conv,
    decay_log,
    decay_bias,
    head_gain,
    out_weight,
    ffn_gain,
    ffn_gate,
    ffn_up,
    ffn_down,
):
    inputs = block_input.astype(jnp.float32)
    cotangent = out_cotangent.astype(jnp.float32)
    local_rows = inputs.shape[0]
    position = lax.axis_index("tensor") * local_rows + jnp.arange(local_rows, dtype=jnp.int32)
    live_rows = (position < lengths[0]).astype(jnp.float32)[:, None]
    query_full, key_full, value_full, gate_full, decay_full, ffn_gate_full, ffn_up_full = (
        lax.all_gather(query_weight, "dp", axis=0, tiled=True),
        lax.all_gather(key_weight, "dp", axis=0, tiled=True),
        lax.all_gather(value_weight, "dp", axis=0, tiled=True),
        lax.all_gather(output_gate_weight, "dp", axis=0, tiled=True),
        lax.all_gather(decay_weight, "dp", axis=0, tiled=True),
        lax.all_gather(ffn_gate, "dp", axis=0, tiled=True),
        lax.all_gather(ffn_up, "dp", axis=0, tiled=True),
    )
    out_full, ffn_down_full = (
        lax.all_gather(out_weight, "dp", axis=1, tiled=True),
        lax.all_gather(ffn_down, "dp", axis=1, tiled=True),
    )
    normed_one, first_back = jax.vjp(rms_scale, inputs, mixer_gain)
    first_rows = group_rows(normed_one.astype(jnp.bfloat16))
    query_pre = matmul(first_rows, query_full)
    key_pre = matmul(first_rows, key_full)
    value_pre = matmul(first_rows, value_full)
    gate_pre = matmul(first_rows, gate_full)
    decay_pre = jnp.einsum(
        "rd,dhc->rhc", first_rows, decay_full, preferred_element_type=jnp.float32
    )
    gated, core_back = jax.vjp(
        mixer_core,
        query_pre,
        key_pre,
        value_pre,
        gate_pre,
        decay_pre,
        query_conv,
        key_conv,
        value_conv,
        decay_log,
        decay_bias,
        head_gain,
    )
    mixed_rows = gated.astype(jnp.bfloat16)
    mixed = row_sums(matmul(mixed_rows, out_full))
    middle = inputs + live_rows * mixed
    normed_two, second_back = jax.vjp(rms_scale, middle, ffn_gain)
    second_rows = group_rows(normed_two.astype(jnp.bfloat16))
    gate_act = matmul(second_rows, ffn_gate_full)
    up_act = matmul(second_rows, ffn_up_full)
    hidden = (jax.nn.silu(gate_act) * up_act).astype(jnp.bfloat16)
    ffn_terms = row_sums(matmul(hidden, ffn_down_full))
    block_output = (middle + live_rows * ffn_terms).astype(jnp.bfloat16)
    fed_grad = group_rows((live_rows * cotangent).astype(jnp.bfloat16))
    hidden_grad = times_transposed(fed_grad, ffn_down_full)
    down_wgrad = contract_rows(hidden, fed_grad)
    sigmoid_gate = jax.nn.sigmoid(gate_act)
    gate_grad = (
        hidden_grad * up_act * sigmoid_gate * (1.0 + gate_act * (1.0 - sigmoid_gate))
    ).astype(jnp.bfloat16)
    up_grad = (hidden_grad * gate_act * sigmoid_gate).astype(jnp.bfloat16)
    gate_wgrad = contract_rows(second_rows, gate_grad)
    up_wgrad = contract_rows(second_rows, up_grad)
    second_in = row_sums(
        times_transposed(gate_grad, ffn_gate_full) + times_transposed(up_grad, ffn_up_full)
    )
    middle_part, ffn_gain_grad = second_back(second_in)
    middle_grad = cotangent + middle_part
    mixed_grad = group_rows((live_rows * middle_grad).astype(jnp.bfloat16))
    gated_grad = times_transposed(mixed_grad, out_full)
    out_wgrad = contract_rows(mixed_rows, mixed_grad)
    (
        query_grad,
        key_grad,
        value_grad,
        gate_pre_grad,
        decay_grad,
        query_conv_grad,
        key_conv_grad,
        value_conv_grad,
        decay_log_grad,
        decay_bias_grad,
        head_gain_grad,
    ) = core_back(gated_grad)
    query_grad = query_grad.astype(jnp.bfloat16)
    key_grad = key_grad.astype(jnp.bfloat16)
    value_grad = value_grad.astype(jnp.bfloat16)
    gate_pre_grad = gate_pre_grad.astype(jnp.bfloat16)
    decay_grad = decay_grad.astype(jnp.bfloat16)
    first_in = (
        times_transposed(query_grad, query_full)
        + times_transposed(key_grad, key_full)
        + times_transposed(value_grad, value_full)
        + times_transposed(gate_pre_grad, gate_full)
        + jnp.einsum("rhc,dhc->rd", decay_grad, decay_full, preferred_element_type=jnp.float32)
    )
    query_wgrad = contract_rows(first_rows, query_grad)
    key_wgrad = contract_rows(first_rows, key_grad)
    value_wgrad = contract_rows(first_rows, value_grad)
    gate_pre_wgrad = contract_rows(first_rows, gate_pre_grad)
    decay_wgrad = jnp.einsum(
        "rd,rhc->dhc", first_rows, decay_grad, preferred_element_type=jnp.float32
    )
    query_sum, key_sum, value_sum, gate_pre_sum, decay_sum, ffn_gate_sum, ffn_up_sum = (
        lax.psum_scatter(
            query_wgrad.astype(jnp.bfloat16), "dp", scatter_dimension=0, tiled=True
        ).astype(jnp.float32),
        lax.psum_scatter(
            key_wgrad.astype(jnp.bfloat16), "dp", scatter_dimension=0, tiled=True
        ).astype(jnp.float32),
        lax.psum_scatter(
            value_wgrad.astype(jnp.bfloat16), "dp", scatter_dimension=0, tiled=True
        ).astype(jnp.float32),
        lax.psum_scatter(
            gate_pre_wgrad.astype(jnp.bfloat16), "dp", scatter_dimension=0, tiled=True
        ).astype(jnp.float32),
        lax.psum_scatter(
            decay_wgrad.astype(jnp.bfloat16), "dp", scatter_dimension=0, tiled=True
        ).astype(jnp.float32),
        lax.psum_scatter(
            gate_wgrad.astype(jnp.bfloat16), "dp", scatter_dimension=0, tiled=True
        ).astype(jnp.float32),
        lax.psum_scatter(
            up_wgrad.astype(jnp.bfloat16), "dp", scatter_dimension=0, tiled=True
        ).astype(jnp.float32),
    )
    out_sum, ffn_down_sum = (
        lax.psum_scatter(
            out_wgrad.astype(jnp.bfloat16), "dp", scatter_dimension=1, tiled=True
        ).astype(jnp.float32),
        lax.psum_scatter(
            down_wgrad.astype(jnp.bfloat16), "dp", scatter_dimension=1, tiled=True
        ).astype(jnp.float32),
    )
    first_sum = row_sums(first_in)
    input_part, mixer_gain_grad = first_back(first_sum)
    input_grad = middle_grad + input_part
    mixer_gain_sum, ffn_gain_sum, head_gain_sum = lax.psum(
        (mixer_gain_grad, ffn_gain_grad, head_gain_grad), ("dp", "tensor")
    )
    query_conv_sum, key_conv_sum, value_conv_sum, decay_log_sum, decay_bias_sum = lax.psum(
        (query_conv_grad, key_conv_grad, value_conv_grad, decay_log_grad, decay_bias_grad), "dp"
    )
    return (
        block_output,
        input_grad,
        mixer_gain_sum,
        query_sum,
        key_sum,
        value_sum,
        gate_pre_sum,
        decay_sum,
        query_conv_sum,
        key_conv_sum,
        value_conv_sum,
        decay_log_sum,
        decay_bias_sum,
        head_gain_sum,
        out_sum,
        ffn_gain_sum,
        ffn_gate_sum,
        ffn_up_sum,
        ffn_down_sum,
    )


def solution(mesh):
    placed = (
        P(("dp", "tensor"), None),
        P(("dp", "tensor"), None),
        P("dp"),
        P(),
        P("dp", "tensor"),
        P("dp", "tensor"),
        P("dp", "tensor"),
        P("dp", "tensor"),
        P("dp", "tensor", None),
        P(None, "tensor"),
        P(None, "tensor"),
        P(None, "tensor"),
        P("tensor"),
        P("tensor"),
        P(),
        P("tensor", "dp"),
        P(),
        P("dp", "tensor"),
        P("dp", "tensor"),
        P("tensor", "dp"),
    )
    return jax.shard_map(
        shards,
        mesh=mesh,
        in_specs=placed,
        out_specs=(
            P(("dp", "tensor"), None),
            P(("dp", "tensor"), None),
            P(),
            P("dp", "tensor"),
            P("dp", "tensor"),
            P("dp", "tensor"),
            P("dp", "tensor"),
            P("dp", "tensor", None),
            P(None, "tensor"),
            P(None, "tensor"),
            P(None, "tensor"),
            P("tensor"),
            P("tensor"),
            P(),
            P("tensor", "dp"),
            P(),
            P("dp", "tensor"),
            P("dp", "tensor"),
            P("tensor", "dp"),
        ),
        check_vma=False,
    )
```

profile of v0, /device:TPU:1, one launch (start us, length us, event | category | flops | bytes accessed | tf_op | source)
XLA Modules:
  0.0 2143.7 jit_solution(1116791945295621928)
XLA Ops:
  9.1 1.9 fusion.202
  12.6 51.6 %all_gather.40 = bf16[1024,1,2]{2,1,0:T(2,128)(2,1)S(1)} all-gather(bf16[64,1,2]{2,1,0:T(2,128)(2,1)S(1)} %copy.99), channel_id=1, replica_groups=mesh['dp'=16,'tensor'=8] {'dp'}, dimensions={0}, use_global_device_ids=true | all-gather | bytes 4352 | tf_op jit(solution)/shard_map/all_gather | solution.py:191
  64.5 21.8 %all_gather.43 = bf16[1024,128]{1,0:T(8,128)(2,1)} all-gather(bf16[64,128]{1,0:T(8,128)(2,1)S(1)} %copy-done.66), channel_id=1, replica_groups=mesh['dp'=16,'tensor'=8] {'dp'}, dimensions={0}, use_global_device_ids=true | all-gather | bytes 278528 | tf_op jit(solution)/shard_map/all_gather | solution.py:187
  86.3 20.9 all_gather.41
  109.0 22.5 %all_gather.42 = bf16[1024,256]{1,0:T(8,128)(2,1)} all-gather(bf16[64,256]{1,0:T(8,128)(2,1)S(1)} %copy-done.57), channel_id=1, replica_groups=mesh['dp'=16,'tensor'=8] {'dp'}, dimensions={0}, use_global_device_ids=true | all-gather | bytes 557056 | tf_op jit(solution)/shard_map/all_gather | solution.py:189
  131.6 23.0 %all_gather.44 = bf16[1024,256]{1,0:T(8,128)(2,1)} all-gather(bf16[64,256]{1,0:T(8,128)(2,1)S(1)} %copy-done.58), channel_id=1, replica_groups=mesh['dp'=16,'tensor'=8] {'dp'}, dimensions={0}, use_global_device_ids=true | all-gather | bytes 557056 | tf_op jit(solution)/shard_map/all_gather | solution.py:190
  154.6 22.5 %all_gather.45 = bf16[256,1024]{0,1:T(8,128)(2,1)} all-gather(bf16[256,64]{0,1:T(8,128)(2,1)S(1)} %copy-done.59), channel_id=1, replica_groups=mesh['dp'=16,'tensor'=8] {'dp'}, dimensions={1}, use_global_device_ids=true | all-gather | bytes 557056 | tf_op jit(solution)/shard_map/all_gather | solution.py:196
  177.1 3.0 convolution_bitcast_fusion.23
  191.5 2.6 fusion.196
  195.4 308.5 %while.44 = (s32[]{:T(128)}, f32[1,256,128]{2,1,0:T(8,128)S(1)}, f32[24,1,64,256]{3,2,1,0:T(8,128)}, f32[24,1,256,128]{3,2,1,0:T(8,128)}, f32[24,1,64]{2,1,0:T(1...) while((s32[]{:T(128)}, f32[1,256,128]{2,1,0:T(8,128)S(1)}, ...), condition=%wide.region_5.6_spmd.clone.clone, body=%wide.region_3.5_spmd.clone.clone.sunk | while | flops 145096704 | bytes 2057661 | solution.py:97
  505.7 3.9 multiply_convert_fusion.3
  510.5 2.7 convolution_convert_fusion
  514.0 38.2 %reduce-scatter.16.cloned.1.call-done = bf16[192,1024]{1,0:T(8,128)(2,1)} async-done(((bf16[1536,1024]{1,0:T(8,128)(2,1)}), bf16[192,1024]{1,0:T(8,128)(2,1)}) %reduce-scatter.16.cloned.1.call-update) | async-done | bytes 393232 | tf_op jit(solution)/shard_map/reduce_scatter | solution.py:154
  554.7 2.2 fusion.204
  557.5 54.7 %all_gather.47 = bf16[1024,352]{1,0:T(8,128)(2,1)} all-gather(bf16[64,352]{1,0:T(8,128)(2,1)} %param.41), channel_id=1, replica_groups=mesh['dp'=16,'tensor'=8] {'dp'}, dimensions={0}, use_global_device_ids=true | all-gather | bytes 765952 | tf_op jit(solution)/shard_map/all_gather | solution.py:192
  612.2 53.3 %all_gather.48 = bf16[1024,352]{1,0:T(8,128)(2,1)} all-gather(bf16[64,352]{1,0:T(8,128)(2,1)} %param.42), channel_id=1, replica_groups=mesh['dp'=16,'tensor'=8] {'dp'}, dimensions={0}, use_global_device_ids=true | all-gather | bytes 765952 | tf_op jit(solution)/shard_map/all_gather | solution.py:193
  665.5 24.2 %all_gather.49 = bf16[352,1024]{0,1:T(8,128)(2,1)} all-gather(bf16[352,64]{0,1:T(8,128)(2,1)S(1)} %copy-done.49), channel_id=1, replica_groups=mesh['dp'=16,'tensor'=8] {'dp'}, dimensions={1}, use_global_device_ids=true | all-gather | bytes 765952 | tf_op jit(solution)/shard_map/all_gather | solution.py:197
  689.7 4.9 fusion.259
  694.6 2.8 fusion.258
  697.3 6.7 multiply_convert_fusion
  704.1 1.9 fusion.260
  706.0 3.6 add_convert_fusion.1
  709.7 40.8 %reduce-scatter.20.cloned.1.call-done = bf16[192,1024]{1,0:T(8,128)(2,1)} async-done(((bf16[1536,1024]{1,0:T(8,128)(2,1)}), bf16[192,1024]{1,0:T(8,128)(2,1)}) %reduce-scatter.20.cloned.1.call-update) | async-done | bytes 393232 | tf_op jit(solution)/shard_map/reduce_scatter | solution.py:154
  750.5 2.2 fusion.205
  753.9 2.4 multiply_convert_fusion.4
  756.4 4.9 convolution_convert_fusion.2
  761.4 4.9 convolution_convert_fusion.3
  766.4 4.9 convolution_convert_fusion.4
  771.6 30.0 %all-gather.11.cloned.1.call-done = bf16[1536,1024]{1,0:T(8,128)(2,1)} async-done(((bf16[192,1024]{1,0:T(8,128)(2,1)}), bf16[1536,1024]{1,0:T(8,128)(2,1)}) %all-gather.11.cloned.1.call-update) | async-done | bytes 3145744 | tf_op jit(solution)/shard_map/all_gather | solution.py:150
  801.5 6.4 multiply_reduce_fusion.4
  807.9 1.8 add_add_fusion
  814.3 772.0 %while.43 = (s32[]{:T(128)}, f32[1,256,128]{2,1,0:T(8,128)}, f32[24,1,64,128]{3,2,1,0:T(8,128)}, f32[24,1,64,128]{3,2,1,0:T(8,128)}, f32[24,1,64,256]{3,2,1,0:T(...) while((s32[]{:T(128)}, f32[1,256,128]{2,1,0:T(8,128)}, ...), condition=%wide.region_25.26_spmd.clone, body=%wide.region_13.25_spmd.clone.sunk | while | flops 372232576 | bytes 6966127 | solution.py:97
  836.1 1.8 fusion.658
  868.3 1.8 fusion.658
  900.6 1.8 fusion.658
  1190.3 1.8 fusion.658
  1286.9 1.8 fusion.658
  1415.7 1.8 fusion.658
  1589.8 2.5 fusion.216
  1592.4 2.4 multiply_reduce_fusion.13
  1596.3 3.7 multiply_reduce_fusion.17
  1603.8 2.1 fusion.215
  1607.7 2.1 fusion.214
  1612.3 4.9 fusion.263
  1617.3 4.3 convolution_convert_fusion.5
  1621.6 4.6 fusion.261
  1626.3 6.5 multiply_reduce_fusion.8
  1632.8 1.9 convolution_convert_fusion.6
  1634.7 4.2 broadcast_multiply_fusion
  1639.2 3.3 fusion.193
  1643.4 1.9 convolution_convert_fusion.7
  1645.2 3.6 fusion.229
  1648.9 3.7 fusion.262
  1652.7 11.3 add_convert_fusion
  1665.4 3.5 convolution_convert_fusion.1
  1674.5 37.4 %all-reduce.32 = (f32[4,128]{1,0:T(4,128)}, f32[4,128]{1,0:T(4,128)}, f32[4,256]{1,0:T(4,128)}, f32[1]{0:T(128)}, f32[1]{0:T(128)}) all-reduce(f32[4,128]{1,0:T(4,128)S(1)} %pad_add_fusion.11, f32[4,128]{1,0:T(4,128)S(1)} %pad_add_fusion.10, f32[4,256]{1,0:T(4,128)S(1)} %pad_add_fusion.9, ...), channel_id=1, replica_groups=mesh['dp'=16,'tensor'=8] {'dp'}, use_global_device_ids=true, to_apply=%region_41.42 | all-reduce | flops 2050 | bytes 16400 | tf_op jit(solution)/shard_map/psum | solution.py:319
  1713.3 24.5 %reduce-scatter.24.cloned.1.call-done = bf16[64,128]{1,0:T(8,128)(2,1)} async-done(((bf16[1024,128]{1,0:T(8,128)(2,1)}), bf16[64,128]{1,0:T(8,128)(2,1)}) %reduce-scatter.24.cloned.1.call-update) | async-done | bytes 16400 | tf_op jit(solution)/shard_map/reduce_scatter | solution.py:283
  1739.2 66.8 %reduce-scatter.26.cloned.1.call-done = bf16[64,128]{1,0:T(8,128)(2,1)} async-done(((bf16[1024,128]{1,0:T(8,128)(2,1)}), bf16[64,128]{1,0:T(8,128)(2,1)}) %reduce-scatter.26.cloned.1.call-update) | async-done | bytes 16400 | tf_op jit(solution)/shard_map/reduce_scatter | solution.py:286
  1807.3 67.4 %reduce-scatter.32.cloned.1.call-done = bf16[256,64]{0,1:T(8,128)(2,1)} async-done(((bf16[256,1024]{0,1:T(8,128)(2,1)}), bf16[256,64]{0,1:T(8,128)(2,1)}) %reduce-scatter.32.cloned.1.call-update) | async-done | bytes 32784 | tf_op jit(solution)/shard_map/reduce_scatter | solution.py:306
  1876.1 66.8 %reduce-scatter.30.cloned.1.call-done = bf16[64,256]{1,0:T(8,128)(2,1)} async-done(((bf16[1024,256]{1,0:T(8,128)(2,1)}), bf16[64,256]{1,0:T(8,128)(2,1)}) %reduce-scatter.30.cloned.1.call-update) | async-done | bytes 32784 | tf_op jit(solution)/shard_map/reduce_scatter | solution.py:292
  1944.3 67.2 %reduce-scatter.28.cloned.1.call-done = bf16[64,256]{1,0:T(8,128)(2,1)} async-done(((bf16[1024,256]{1,0:T(8,128)(2,1)}), bf16[64,256]{1,0:T(8,128)(2,1)}) %reduce-scatter.28.cloned.1.call-update) | async-done | bytes 32784 | tf_op jit(solution)/shard_map/reduce_scatter | solution.py:289
  2012.9 43.9 %reduce-scatter.22.cloned.1.call-done = bf16[192,1024]{1,0:T(8,128)(2,1)} async-done(((bf16[1536,1024]{1,0:T(8,128)(2,1)}), bf16[192,1024]{1,0:T(8,128)(2,1)}) %reduce-scatter.22.cloned.1.call-update) | async-done | bytes 393232 | tf_op jit(solution)/shard_map/reduce_scatter | solution.py:154
  2058.2 75.7 %all-reduce.31 = (f32[1024]{0:T(1024)}, f32[256]{0:T(256)}, f32[1024]{0:T(1024)}) all-reduce(f32[1024]{0:T(1024)S(1)} %get-tuple-element.718, f32[256]{0:T(256)S(1)} %copy-done.108, f32[1024]{0:T(1024)S(1)} %copy-done.65), channel_id=1, replica_groups=mesh['dp'=16,'tensor'=8] {'dp','tensor'}, use_global_device_ids=true, to_apply=%region_31.32 | all-reduce | flops 2304 | bytes 18432 | tf_op jit(solution)/shard_map/psum | solution.py:316
  2134.0 2.8 fusion.211
  (2630 shorter events, 1117.0 us)
Async XLA Ops:
  7.2 57.3 %copy-start.66 = (bf16[64,128]{1,0:T(8,128)(2,1)S(1)}, bf16[64,128]{1,0:T(8,128)(2,1)}, u32[]{:S(2)}) copy-start(bf16[64,128]{1,0:T(8,128)(2,1)} %param.28) | copy-start | bytes 49156
  7.2 79.1 %copy-start.67 = (bf16[64,128]{1,0:T(8,128)(2,1)S(1)}, bf16[64,128]{1,0:T(8,128)(2,1)}, u32[]{:S(2)}) copy-start(bf16[64,128]{1,0:T(8,128)(2,1)} %param.29) | copy-start | bytes 49156
  7.2 100.0 %copy-start.98 = (f32[4,128]{1,0:T(4,128)S(1)}, f32[4,128]{1,0:T(4,128)}, u32[]{:S(2)}) copy-start(f32[4,128]{1,0:T(4,128)} %param.33) | copy-start | bytes 6148
  7.2 100.6 %copy-start.99 = (f32[4,128]{1,0:T(4,128)S(1)}, f32[4,128]{1,0:T(4,128)}, u32[]{:S(2)}) copy-start(f32[4,128]{1,0:T(4,128)} %param.34) | copy-start | bytes 6148
  7.2 101.2 %copy-start.97 = (f32[4,256]{1,0:T(4,128)S(1)}, f32[4,256]{1,0:T(4,128)}, u32[]{:S(2)}) copy-start(f32[4,256]{1,0:T(4,128)} %param.35) | copy-start | bytes 12292
  7.3 101.8 %copy-start.57 = (bf16[64,256]{1,0:T(8,128)(2,1)S(1)}, bf16[64,256]{1,0:T(8,128)(2,1)}, u32[]{:S(2)}) copy-start(bf16[64,256]{1,0:T(8,128)(2,1)} %param.30) | copy-start | bytes 98308
  7.3 169.8 %all-gather.5.cloned.1.call-start = ((), (), s32[]{:S(2)}) async-start(), calls=%async_computation.13 | async-start | bytes 3538944 | tf_op jit(solution)/shard_map/all_gather | solution.py:150
  9.1 122.5 %copy-start.58 = (bf16[64,256]{1,0:T(8,128)(2,1)S(1)}, bf16[64,256]{1,0:T(8,128)(2,1)}, u32[]{:S(2)}) copy-start(bf16[64,256]{1,0:T(8,128)(2,1)} %param.31) | copy-start | bytes 98308
  11.0 143.6 %copy-start.59 = (bf16[256,64]{0,1:T(8,128)(2,1)S(1)}, bf16[256,64]{0,1:T(8,128)(2,1)}, u32[]{:S(2)}) copy-start(bf16[256,64]{0,1:T(8,128)(2,1)} %param.39) | copy-start | bytes 98308
  11.0 541.3 %reduce-scatter.16.cloned.1.call-start = ((), (), s32[]{:S(2)}) async-start(), calls=%async_computation.14 | async-start | bytes 3538944 | tf_op jit(solution)/shard_map/reduce_scatter | solution.py:154
  64.5 115.5 %copy-start.51 = (bf16[1024,1,2]{0,2,1:T(2,128)(2,1)}, bf16[1024,1,2]{0,2,1:T(2,128)(2,1)S(1)}, u32[]{:S(2)}) copy-start(bf16[1024,1,2]{0,2,1:T(2,128)(2,1)S(1)} %copy.100) | copy-start | bytes 12292
  107.2 76.1 %copy-start.26 = (bf16[1024,128]{1,0:T(8,128)(2,1)}, bf16[1024,128]{1,0:T(8,128)(2,1)S(1)}, u32[]{:S(2)}) copy-start(bf16[1024,128]{1,0:T(8,128)(2,1)S(1)} %all_gather.41) | copy-start | bytes 786436
  109.0 82.4 %copy-start.73 = (f32[1,256]{1,0:T(1,128)}, f32[1,256]{1,0:T(1,128)S(1)}, u32[]{:S(2)}) copy-start(f32[1,256]{1,0:T(1,128)S(1)} %get-tuple-element.831) | copy-start | bytes 3076
  513.2 39.0 %copy-start.2 = (bf16[192,1024]{1,0:T(8,128)(2,1)S(1)}, bf16[192,1024]{1,0:T(8,128)(2,1)}, u32[]{:S(2)}) copy-start(bf16[192,1024]{1,0:T(8,128)(2,1)} %param.24) | copy-start | bytes 1179652
  513.2 41.4 %copy-start.47 = (f32[1024]{0:T(1024)S(1)}, f32[1024]{0:T(1024)}, u32[]{:S(2)}) copy-start(f32[1024]{0:T(1024)} %param.40) | copy-start | bytes 12292
  513.3 176.4 %all-gather.7.cloned.1.call-start = ((), (), s32[]{:S(2)}) async-start(), calls=%async_computation.15 | async-start | bytes 3538944 | tf_op jit(solution)/shard_map/all_gather | solution.py:150
  514.0 239.3 %copy-start.53 = (f32[192]{0:T(256)}, f32[192]{0:T(256)S(1)}, u32[]{:S(2)}) copy-start(f32[192]{0:T(256)S(1)} %compare_convert_fusion) | copy-start | bytes 2308
  556.9 140.5 %all-gather.9.cloned.1.call-start = ((), (), s32[]{:S(2)}) async-start(), calls=%async_computation.17 | async-start | bytes 3538944 | tf_op jit(solution)/shard_map/all_gather | solution.py:150
  557.4 193.0 %reduce-scatter.20.cloned.1.call-start = ((), (), s32[]{:S(2)}) async-start(), calls=%async_computation.18 | async-start | bytes 3538944 | tf_op jit(solution)/shard_map/reduce_scatter | solution.py:154
  557.5 108.0 %copy-start.49 = (bf16[352,64]{0,1:T(8,128)(2,1)S(1)}, bf16[352,64]{0,1:T(8,128)(2,1)}, u32[]{:S(2)}) copy-start(bf16[352,64]{0,1:T(8,128)(2,1)} %param.43) | copy-start | bytes 135172
  709.6 91.9 %all-gather.11.cloned.1.call-start = ((), (), s32[]{:S(2)}) async-start(), calls=%async_computation.19 | async-start | bytes 3538944 | tf_op jit(solution)/shard_map/all_gather | solution.py:150
  756.3 912.9 %reduce-scatter.38.cloned.1.call-start = ((), (), s32[]{:S(2)}) async-start(), calls=%async_computation.28 | async-start | bytes 835584 | tf_op jit(solution)/shard_map/reduce_scatter | solution.py:309
  761.3 909.5 %reduce-scatter.36.cloned.1.call-start = ((), (), s32[]{:S(2)}) async-start(), calls=%async_computation.27 | async-start | bytes 835584 | tf_op jit(solution)/shard_map/reduce_scatter | solution.py:301
  766.3 905.9 %reduce-scatter.34.cloned.1.call-start = ((), (), s32[]{:S(2)}) async-start(), calls=%async_computation.26 | async-start | bytes 835584 | tf_op jit(solution)/shard_map/reduce_scatter | solution.py:298
  766.4 35.1 %copy-start.56 = (f32[1536]{0:T(1024)S(1)}, f32[1536]{0:T(1024)}, u32[]{:S(2)}) copy-start(f32[1536]{0:T(1024)} %copy-done.55) | copy-start | bytes 18436
  766.4 35.1 %copy-start.110 = (f32[256]{0:T(256)S(1)}, f32[256]{0:T(256)}, u32[]{:S(2)}) copy-start(f32[256]{0:T(256)} %param.38) | copy-start | bytes 3076
  771.3 940.6 %reduce-scatter.40.cloned.1.call-start = ((), (), s32[]{:S(2)}) async-start(), calls=%async_computation.29 | async-start | bytes 278528
  824.5 7.7 copy-start.13
  856.6 7.7 copy-start.13
  888.9 7.7 copy-start.13
  921.1 7.7 copy-start.13
  953.3 7.7 copy-start.13
  1017.7 7.7 copy-start.13
  1049.9 7.7 copy-start.13
  1114.2 7.7 copy-start.13
  1146.4 7.7 copy-start.13
  1178.6 7.7 copy-start.13
  1210.8 7.7 copy-start.13
  1243.0 7.7 copy-start.13
  1275.2 7.7 copy-start.13
  1307.5 7.7 copy-start.13
  1339.7 7.7 copy-start.13
  1468.5 7.7 copy-start.13
  1532.9 7.7 copy-start.13
  1603.6 134.2 %reduce-scatter.24.cloned.1.call-start = ((), (), s32[]{:S(2)}) async-start(), calls=%async_computation.21 | async-start | bytes 278528 | tf_op jit(solution)/shard_map/reduce_scatter | solution.py:283
  1607.7 198.3 %reduce-scatter.26.cloned.1.call-start = ((), (), s32[]{:S(2)}) async-start(), calls=%async_computation.22 | async-start | bytes 278528 | tf_op jit(solution)/shard_map/reduce_scatter | solution.py:286
  1617.3 257.4 %reduce-scatter.32.cloned.1.call-start = ((), (), s32[]{:S(2)}) async-start(), calls=%async_computation.25 | async-start | bytes 557056 | tf_op jit(solution)/shard_map/reduce_scatter | solution.py:306
  1626.2 316.7 %reduce-scatter.30.cloned.1.call-start = ((), (), s32[]{:S(2)}) async-start(), calls=%async_computation.24 | async-start | bytes 557056 | tf_op jit(solution)/shard_map/reduce_scatter | solution.py:292
  1638.9 372.7 %reduce-scatter.28.cloned.1.call-start = ((), (), s32[]{:S(2)}) async-start(), calls=%async_computation.23 | async-start | bytes 557056 | tf_op jit(solution)/shard_map/reduce_scatter | solution.py:289
  1652.6 404.2 %reduce-scatter.22.cloned.1.call-start = ((), (), s32[]{:S(2)}) async-start(), calls=%async_computation.20 | async-start | bytes 3538944 | tf_op jit(solution)/shard_map/reduce_scatter | solution.py:154
  1664.0 469.9 %reduce-scatter.18.cloned.1.call-start = ((), (), s32[]{:S(2)}) async-start(), calls=%async_computation.16 | async-start | bytes 3538944 | tf_op jit(solution)/shard_map/reduce_scatter | solution.py:154
  1669.0 387.8 %copy-start.3 = (bf16[192,1024]{1,0:T(8,128)(2,1)S(1)}, bf16[192,1024]{1,0:T(8,128)(2,1)}, u32[]{:S(2)}) copy-start(bf16[192,1024]{1,0:T(8,128)(2,1)} %param.24) | copy-start | bytes 1179652
  1669.0 387.8 %copy-start.50 = (f32[1024]{0:T(1024)S(1)}, f32[1024]{0:T(1024)}, u32[]{:S(2)}) copy-start(f32[1024]{0:T(1024)} %param.27) | copy-start | bytes 12292
  1669.0 387.8 %copy-start.64 = (f32[192]{0:T(256)S(1)}, f32[192]{0:T(256)}, u32[]{:S(2)}) copy-start(f32[192]{0:T(256)} %copy-done.63) | copy-start | bytes 2308
  1669.0 389.1 %copy-start.65 = (f32[1024]{0:T(1024)S(1)}, f32[1024]{0:T(1024)}, u32[]{:S(2)}) copy-start(f32[1024]{0:T(1024)} %get-tuple-element.716) | copy-start | bytes 12292
  1669.1 389.1 %copy-start.108 = (f32[256]{0:T(256)S(1)}, f32[256]{0:T(256)}, u32[]{:S(2)}) copy-start(f32[256]{0:T(256)} %get-tuple-element.702) | copy-start | bytes 3076
  1669.1 464.8 %copy-start.71 = (f32[192]{0:T(256)S(1)}, f32[192]{0:T(256)}, u32[]{:S(2)}) copy-start(f32[192]{0:T(256)} %copy-done.70) | copy-start | bytes 2308
  1669.1 464.8 %copy-start.8 = (bf16[192,1024]{1,0:T(8,128)(2,1)S(1)}, bf16[192,1024]{1,0:T(8,128)(2,1)}, u32[]{:S(2)}) copy-start(bf16[192,1024]{1,0:T(8,128)(2,1)} %reduce-scatter.16.cloned.1.call-done) | copy-start | bytes 1179652
  1669.1 464.8 %copy-start.18 = (bf16[192,1024]{1,0:T(8,128)(2,1)S(1)}, bf16[192,1024]{1,0:T(8,128)(2,1)}, u32[]{:S(2)}) copy-start(bf16[192,1024]{1,0:T(8,128)(2,1)} %param.25) | copy-start | bytes 1179652
  1669.1 464.8 %copy-start.19 = (bf16[192,1024]{1,0:T(8,128)(2,1)S(1)}, bf16[192,1024]{1,0:T(8,128)(2,1)}, u32[]{:S(2)}) copy-start(bf16[192,1024]{1,0:T(8,128)(2,1)} %reduce-scatter.20.cloned.1.call-done) | copy-start | bytes 1179652
  1669.1 464.8 %copy-start.48 = (f32[1024]{0:T(1024)S(1)}, f32[1024]{0:T(1024)}, u32[]{:S(2)}) copy-start(f32[1024]{0:T(1024)} %param.40) | copy-start | bytes 12292
  1669.1 464.8 %copy-start.54 = (f32[192]{0:T(256)S(1)}, f32[192]{0:T(256)}, u32[]{:S(2)}) copy-start(f32[192]{0:T(256)} %copy-done.53) | copy-start | bytes 2308
  1669.1 464.8 %copy-start.61 = (f32[192]{0:T(256)S(1)}, f32[192]{0:T(256)}, u32[]{:S(2)}) copy-start(f32[192]{0:T(256)} %copy-done.60) | copy-start | bytes 2308
  1669.1 464.8 %copy-start.69 = (f32[192]{0:T(256)S(1)}, f32[192]{0:T(256)}, u32[]{:S(2)}) copy-start(f32[192]{0:T(256)} %copy-done.68) | copy-start | bytes 2308
  (136 other events, 320.7 us)
Sparse Core Ops, SparseCore 0:
  11.1 44.9 all-gather.4
  513.4 38.8 reduce-scatter.15
  557.0 45.0 all-gather.6
  604.2 43.9 all-gather.8
  709.7 40.6 reduce-scatter.19
  756.4 45.0 all-gather.10
  805.3 66.9 reduce-scatter.37
  876.6 65.3 reduce-scatter.35
  945.8 65.4 reduce-scatter.33
  1603.7 65.7 reduce-scatter.39
  1673.6 64.1 reduce-scatter.23
  1741.8 64.1 reduce-scatter.25
  1810.1 64.5 reduce-scatter.31
  1878.3 64.5 reduce-scatter.29
  1946.9 64.5 reduce-scatter.27
  2013.8 42.9 reduce-scatter.21
  2059.1 46.0 reduce-scatter.17
where the time goes:
time: 2170 us; the launch traced here: 2140 us
  matrix products  766 us (35%)
  waiting for transfers between devices  447 us (21%)
  blocking collectives  408 us (19%)
  other arithmetic  269 us (12%)
  local copies, waits for them, and re-layouts  223 us (10%)
    dot_general x1560, matrix products, exact_dot(): return jnp.dot(left_side, right_side, precision=lax.Precision.HIGHEST)  669 us
    reduce_scatter x4, waiting for transfers between devices, row_sums(): lax.psum_scatter(values.astype(jnp.bfloat16), 'tensor', scatter_dimension...  123 us
    squeeze x120, local copies, waits for them, and re-layouts, delta_head(): lax.scan(jax.checkpoint(block_step), start_memory, (into_blocks(queries),...  109 us
    psum x1, blocking collectives, shards(): lax.psum((mixer_gain_grad, ffn_gain_grad, head_gain_grad), ('dp', 'tensor'))  75.7 us
    reduce_scatter x1, waiting for transfers between devices, shards(): lax.psum_scatter(out_wgrad.astype(jnp.bfloat16), 'dp', scatter_dimension=...  67.4 us
    reduce_scatter x1, waiting for transfers between devices, shards(): lax.psum_scatter(value_wgrad.astype(jnp.bfloat16), 'dp', scatter_dimensio...  67.2 us
    reduce_scatter x1, waiting for transfers between devices, shards(): lax.psum_scatter(key_wgrad.astype(jnp.bfloat16), 'dp', scatter_dimension=...  66.8 us
    reduce_scatter x1, waiting for transfers between devices, shards(): lax.psum_scatter(gate_pre_wgrad.astype(jnp.bfloat16), 'dp', scatter_dimen...  66.8 us
  transfers between devices with their start and end apart: 17, of which 9 were waited for; matrix products, arithmetic and copies ran while one was open for 41% of the time, Pallas kernels for 0%

commit v1 on v0

v1 whole, which is shorter than its diff:
```python
import functools

import jax
import jax.numpy as jnp
from jax import lax
from jax.experimental import pallas as pl
from jax.experimental.pallas import tpu as pltpu
from jax.sharding import PartitionSpec as P

DK = 128
DV = 256
QKV = 2 * DK + DV
D = 1024
CHUNK = 256
BATCH = 2

norm_eps = 1e-06
gate_eps = 1e-05
bf16 = jnp.bfloat16
f32 = jnp.float32


def mm(left_side, right_side, left_dim=1, right_dim=0):
    return lax.dot_general(
        left_side.astype(bf16),
        right_side.astype(bf16),
        (((left_dim,), (right_dim,)), ((), ())),
        preferred_element_type=f32,
    )


def halves(values):
    high = values.astype(bf16)
    return high, (values - high.astype(f32)).astype(bf16)


def mm3(left_pair, right_pair, left_dim=1, right_dim=0):
    (lh, ll), (rh, rl) = left_pair, right_pair
    return (
        mm(lh, rh, left_dim, right_dim)
        + mm(lh, rl, left_dim, right_dim)
        + mm(ll, rh, left_dim, right_dim)
    )


def ones_mm(ones_side, values, terms):
    total = None
    for _ in range(terms):
        high = values.astype(bf16)
        part = mm(ones_side, high)
        total = part if total is None else total + part
        values = values - high.astype(f32)
    return total


def wide(lanes):
    return jnp.concatenate([lanes, lanes], axis=1)


def row_total(values):
    return jnp.sum(values, axis=-1, keepdims=True)


def softplus(z):
    return jnp.maximum(z, 0.0) + jnp.log1p(jnp.exp(-jnp.abs(z)))


def index_pair():
    return (
        lax.broadcasted_iota(jnp.int32, (CHUNK, CHUNK), 0),
        lax.broadcasted_iota(jnp.int32, (CHUNK, CHUNK), 1),
    )


def taps_sum(conv_ref, pad_ref, start):
    total = None
    for tap in range(4):
        term = conv_ref[tap : tap + 1, :] * pad_ref[pl.ds(start + 5 + tap, CHUNK), :]
        total = term if total is None else total + term
    return total


def gates(decay_pre, write_pre, dec_ref):
    z = decay_pre + dec_ref[1:2, :]
    return z, dec_ref[0:1, :] * softplus(z), jax.nn.sigmoid(write_pre)


def cumulative(decays, causal_ones):
    total = ones_mm(causal_ones, decays, 3)
    across = jnp.transpose(total)[0:1, :]
    return total, across


def ratios(total, across, causal):
    spread = wide(total) - across
    return jnp.where(causal, jnp.exp(jnp.where(causal, spread, 0.0)), 0.0)


def mix_forward(
    first_ref, wall_ref, conv_ref, dec_ref, hg_ref, out_ref,
    proj_ref, part_ref, mixed_ref, o_ref, t_ref, u_ref, w_ref, qe_ref, a_ref, s_ref, tail_ref,
    state, pad,
):
    @pl.when(pl.program_id(0) == 0)
    def _():
        state[...] = jnp.zeros_like(state)
        pad[0:8, :] = jnp.zeros((8, QKV), f32)

    row, col = index_pair()
    causal = row >= col
    strict = row > col
    causal_ones = causal.astype(bf16)
    parts = range(BATCH)
    rows = [pl.ds(c * CHUNK, CHUNK) for c in parts]
    for c in parts:
        pre = mm(first_ref[rows[c], :], wall_ref[...])
        proj_ref[rows[c], :] = pre
        pad[pl.ds(8 + c * CHUNK, CHUNK), :] = pre[:, :QKV]
    items = []
    for c in parts:
        tail_ref[c] = pad[pl.ds(c * CHUNK, 8), :]
        act = jax.nn.silu(taps_sum(conv_ref, pad, c * CHUNK))
        q, k, v = act[:, :DK], act[:, DK : 2 * DK], act[:, 2 * DK :]
        q = q * (lax.rsqrt(row_total(q * q) + norm_eps) * DK ** (-0.5))
        k = k * lax.rsqrt(row_total(k * k) + norm_eps)
        _, decays, rate = gates(
            proj_ref[rows[c], 768:896], proj_ref[rows[c], 896:1024], dec_ref
        )
        total, across = cumulative(decays, causal_ones)
        ratio = ratios(total, across, causal)
        kk = mm(k, k, 1, 1)
        lower = jnp.where(strict, wide(rate) * kk * ratio, 0.0)
        scores = (mm(q, k, 1, 1) * ratio).astype(bf16)
        growth = jnp.exp(total)
        last = total[CHUNK - 1 : CHUNK, :]
        tail_k = (jnp.exp(last - total) * k).astype(bf16)
        items.append((q, k, v, rate, growth, jnp.exp(last), tail_k, scores, lower))
    pad[0:8, :] = pad[pl.ds(BATCH * CHUNK, 8), :]
    size = 1
    inverse = [(row == col).astype(f32) for c in parts]
    while size < CHUNK:
        same = (row // (2 * size) == col // (2 * size)) & ((row // size) % 2 == 1) & ((col // size) % 2 == 0)
        for c in parts:
            edge = jnp.where(same, items[c][8], 0.0)
            if size == 1:
                inverse[c] = inverse[c] - edge
            else:
                pair = halves(inverse[c])
                inverse[c] = inverse[c] - mm3(halves(mm3(pair, halves(edge))), pair)
        size *= 2
    eye = lax.broadcasted_iota(jnp.int32, (DK, DK), 0) == lax.broadcasted_iota(
        jnp.int32, (DK, DK), 1
    )
    later = []
    for c in parts:
        q, k, v, rate, growth, grown, tail_k, scores, _ = items[c]
        solve = inverse[c].astype(bf16)
        t_ref[c] = solve
        w = mm(solve, rate * growth * k).astype(bf16)
        u_start = mm(solve, wide(rate) * v)
        q_eff = (growth * q - mm(scores, w)).astype(bf16)
        carry = jnp.where(eye, grown, 0.0) - mm(w, tail_k, 0, 0)
        added = mm(u_start, tail_k, 0, 0)
        w_ref[c] = w
        qe_ref[c] = q_eff
        a_ref[c] = carry
        later.append((w, u_start, q_eff, scores, carry, added))
    memory = state[...]
    starts = []
    for c in parts:
        s_ref[c] = memory
        starts.append(memory)
        memory = mm(memory, later[c][4]) + later[c][5]
    state[...] = memory
    for c in parts:
        w, u_start, q_eff, scores, _, _ = later[c]
        u_ref[c] = (u_start - mm(w, starts[c], 1, 1)).astype(bf16)
        o = mm(q_eff, starts[c], 1, 1) + mm(scores, u_start)
        o_ref[rows[c], :] = o
        normed = o * lax.rsqrt(row_total(o * o) * (1.0 / DV) + gate_eps) * hg_ref[...]
        mixed = (normed * jax.nn.silu(proj_ref[rows[c], 512:768])).astype(bf16)
        mixed_ref[rows[c], :] = mixed
        part_ref[rows[c], :] = mm(mixed, out_ref[...], 1, 1).astype(bf16)


def mix_backward(
    grad_ref, out_ref, proj_ref, tail_ref, o_ref, t_ref, u_ref, w_ref, qe_ref, a_ref, s_ref,
    wall_ref, conv_ref, dec_ref, hg_ref,
    pre_ref, first_ref, conv_grad_ref, small_ref,
    dstate, padp, padg,
):
    @pl.when(pl.program_id(0) == 0)
    def _():
        dstate[...] = jnp.zeros_like(dstate)
        padg[pl.ds(BATCH * CHUNK, 8), :] = jnp.zeros((8, QKV), f32)
        conv_grad_ref[...] = jnp.zeros_like(conv_grad_ref)
        small_ref[...] = jnp.zeros_like(small_ref)

    row, col = index_pair()
    causal = row >= col
    strict = row > col
    causal_ones = causal.astype(bf16)
    strict_ones = strict.astype(bf16)
    upper_ones = (col >= row).astype(bf16)
    lane = lax.broadcasted_iota(jnp.int32, (CHUNK, DK), 1)
    parts = range(BATCH)
    rows = [pl.ds(c * CHUNK, CHUNK) for c in parts]
    padp[0:8, :] = tail_ref[0]
    for c in parts:
        padp[pl.ds(8 + c * CHUNK, CHUNK), :] = proj_ref[rows[c], :QKV]
    items = []
    for c in parts:
        act_pre = taps_sum(conv_ref, padp, c * CHUNK)
        act_sig = jax.nn.sigmoid(act_pre)
        act = act_pre * act_sig
        slope = act_sig * (1.0 + act_pre * (1.0 - act_sig))
        qc, kc, v = act[:, :DK], act[:, DK : 2 * DK], act[:, 2 * DK :]
        q_scale = lax.rsqrt(row_total(qc * qc) + norm_eps)
        k_scale = lax.rsqrt(row_total(kc * kc) + norm_eps)
        q = qc * (q_scale * DK ** (-0.5))
        k = kc * k_scale
        z, decays, rate = gates(
            proj_ref[rows[c], 768:896], proj_ref[rows[c], 896:1024], dec_ref
        )
        total, across = cumulative(decays, causal_ones)
        ratio = ratios(total, across, causal)
        key_ratio = mm(k, k, 1, 1) * ratio
        scores = mm(q, k, 1, 1) * ratio
        growth = jnp.exp(total)
        last = total[CHUNK - 1 : CHUNK, :]
        tail = jnp.exp(last - total)
        grad = mm(grad_ref[rows[c], :], out_ref[...])
        gate = proj_ref[rows[c], 512:768]
        gate_sig = jax.nn.sigmoid(gate)
        gate_act = gate * gate_sig
        o = o_ref[rows[c], :]
        o_scale = lax.rsqrt(row_total(o * o) * (1.0 / DV) + gate_eps)
        normed = o * o_scale
        gain = hg_ref[...]
        gate_grad = grad * normed * gain * gate_sig * (1.0 + gate * (1.0 - gate_sig))
        pre_ref[rows[c], 512:768] = gate_grad.astype(bf16)
        grad = grad * gate_act
        small_ref[0:1, :] += jnp.sum(grad * normed, axis=0, keepdims=True)
        grad = grad * gain
        do = o_scale * (grad - normed * (row_total(grad * normed) * (1.0 / DV)))
        do = do.astype(bf16)
        items.append(
            (slope, q, k, v, q_scale, k_scale, z, decays, rate, ratio, key_ratio, scores,
             growth, jnp.exp(last), tail, do)
        )
    ends = [None] * BATCH
    change = dstate[...]
    for c in reversed(parts):
        ends[c] = change
        change = mm(change, a_ref[c], 1, 1) + mm(items[c][15], qe_ref[c], 0, 0)
    dstate[...] = change
    for c in reversed(parts):
        (slope, q, k, v, q_scale, k_scale, z, decays, rate, ratio, key_ratio, scores,
         growth, grown, tail, do) = items[c]
        start = s_ref[c]
        end = ends[c]
        start16 = start.astype(bf16)
        end16 = end.astype(bf16)
        u = u_ref[c]
        q16, k16 = q.astype(bf16), k.astype(bf16)
        du = mm(scores, do, 0, 0) + mm(tail * k, end16, 1, 1)
        dx = mm(t_ref[c], du, 0, 0)
        dx16 = dx.astype(bf16)
        d_scores = jnp.where(causal, mm(do, u, 1, 1), 0.0)
        d_lower = jnp.where(strict, -mm(dx16, u, 1, 1), 0.0)
        score_side = (d_scores * ratio).astype(bf16)
        rate2 = wide(rate)
        growth2 = wide(growth)
        lower_keys = d_lower * key_ratio
        key_side = (d_lower * rate2 * ratio).astype(bf16)
        do_state = mm(do, start16)
        dx_state = mm(dx16, start16)
        u_state = mm(u, end16)
        key_state = mm(k16, start16, 1, 1)
        dq = growth * do_state + mm(score_side, k16)
        rate_growth = rate * growth
        dk = (
            mm(score_side, q16, 0, 0)
            + mm(key_side, k16)
            + mm(key_side, k16, 0, 0)
            - rate_growth * dx_state
            + tail * u_state
        )
        dv = rate2 * dx
        d_rate = row_total(lower_keys) + row_total(dx * (v - growth2 * key_state))
        from_growth = row_total(growth * q * do_state - rate_growth * k * dx_state)
        from_tail = row_total(tail * k * u_state)
        pairs = d_scores * scores + rate2 * lower_keys
        held = ones_mm(upper_ones, pairs, 2)
        spread_growth = ones_mm(upper_ones, jnp.broadcast_to(from_growth, (CHUNK, DK)), 2)
        spread_tail = ones_mm(strict_ones, jnp.broadcast_to(from_tail, (CHUNK, DK)), 2)
        through = jnp.sum(row_total(end * start), axis=0, keepdims=True)
        d_decay = (
            row_total(jnp.where(strict, held, 0.0))
            + spread_growth
            + spread_tail
            + grown * through
        )
        dz = d_decay * dec_ref[0:1, :] * jax.nn.sigmoid(z)
        d_write = d_rate * rate * (1.0 - rate)
        pre_ref[rows[c], 768:896] = jnp.where(
            lane == 0, dz, jnp.where(lane == 1, d_write, 0.0)
        ).astype(bf16)
        small_ref[1:2, :DK] += jnp.sum(d_decay * decays, axis=0, keepdims=True)
        small_ref[2:3, :DK] += jnp.sum(dz, axis=0, keepdims=True)
        dqc = q_scale * (DK ** (-0.5) * dq - q * (row_total(q * dq) * DK**0.5))
        dkc = k_scale * (dk - k * row_total(k * dk))
        dact = jnp.concatenate([dqc, dkc, dv], axis=1) * slope
        padg[pl.ds(c * CHUNK, CHUNK), :] = dact
        dpre = None
        for tap in range(4):
            weight = conv_ref[tap : tap + 1, :]
            term = weight * padg[pl.ds(c * CHUNK + 3 - tap, CHUNK), :]
            dpre = term if dpre is None else dpre + term
            conv_grad_ref[tap : tap + 1, :] += jnp.sum(
                dact * padp[pl.ds(c * CHUNK + 5 + tap, CHUNK), :], axis=0, keepdims=True
            )
        pre_ref[rows[c], :QKV] = dpre.astype(bf16)
        first_ref[rows[c], :] = mm(pre_ref[rows[c], :], wall_ref[...], 1, 1).astype(bf16)
    padg[pl.ds(BATCH * CHUNK, 8), :] = padg[0:8, :]


def call_forward(first_rows, wall, conv, dec, hg, out_t):
    rows = first_rows.shape[0]
    chunks = rows // CHUNK
    steps = chunks // BATCH
    tall = lambda width: pl.BlockSpec((BATCH * CHUNK, width), lambda i: (i, 0))
    fixed = lambda shape: pl.BlockSpec(shape, lambda i: (0, 0))
    per = lambda *shape: pl.BlockSpec((BATCH,) + shape, lambda i: (i, 0, 0))
    made = jax.ShapeDtypeStruct
    return pl.pallas_call(
        mix_forward,
        grid=(steps,),
        in_specs=[
            tall(D), fixed((D, 1024)), fixed((8, QKV)), fixed((8, DK)), fixed((1, DV)),
            fixed((D, DV)),
        ],
        out_specs=[
            tall(1024), tall(D), tall(DV), tall(DV), per(CHUNK, CHUNK), per(CHUNK, DV),
            per(CHUNK, DK), per(CHUNK, DK), per(DK, DK), per(DV, DK), per(8, QKV),
        ],
        out_shape=[
            made((rows, 1024), f32), made((rows, D), bf16), made((rows, DV), bf16),
            made((rows, DV), f32), made((chunks, CHUNK, CHUNK), bf16),
            made((chunks, CHUNK, DV), bf16), made((chunks, CHUNK, DK), bf16),
            made((chunks, CHUNK, DK), bf16), made((chunks, DK, DK), f32),
            made((chunks, DV, DK), f32), made((chunks, 8, QKV), f32),
        ],
        scratch_shapes=[
            pltpu.VMEM((DV, DK), f32), pltpu.VMEM((BATCH * CHUNK + 8, QKV), f32),
        ],
        compiler_params=pltpu.CompilerParams(
            dimension_semantics=("arbitrary",), vmem_limit_bytes=56 * 1024 * 1024
        ),
        cost_estimate=pl.CostEstimate(
            flops=30_000_000_000, bytes_accessed=20_000_000, transcendentals=4_000_000
        ),
        name="mix_forward",
    )(first_rows, wall, conv, dec, hg, out_t)


def call_backward(grad_rows, out_t, saved, wall, conv, dec, hg):
    proj, o, t, u, w, qe, a, s, tails = saved
    rows = grad_rows.shape[0]
    chunks = rows // CHUNK
    steps = chunks // BATCH
    tall = lambda width: pl.BlockSpec((BATCH * CHUNK, width), lambda i: (steps - 1 - i, 0))
    fixed = lambda shape: pl.BlockSpec(shape, lambda i: (0, 0))
    per = lambda *shape: pl.BlockSpec((BATCH,) + shape, lambda i: (steps - 1 - i, 0, 0))
    made = jax.ShapeDtypeStruct
    return pl.pallas_call(
        mix_backward,
        grid=(steps,),
        in_specs=[
            tall(D), fixed((D, DV)), tall(1024), per(8, QKV), tall(DV), per(CHUNK, CHUNK),
            per(CHUNK, DV), per(CHUNK, DK), per(CHUNK, DK), per(DK, DK), per(DV, DK),
            fixed((D, 896)), fixed((8, QKV)), fixed((8, DK)), fixed((1, DV)),
        ],
        out_specs=[tall(896), tall(D), fixed((8, QKV)), fixed((8, DV))],
        out_shape=[
            made((rows, 896), bf16), made((rows, D), bf16), made((8, QKV), f32),
            made((8, DV), f32),
        ],
        scratch_shapes=[
            pltpu.VMEM((DV, DK), f32), pltpu.VMEM((BATCH * CHUNK + 8, QKV), f32),
            pltpu.VMEM((BATCH * CHUNK + 8, QKV), f32),
        ],
        compiler_params=pltpu.CompilerParams(
            dimension_semantics=("arbitrary",), vmem_limit_bytes=56 * 1024 * 1024
        ),
        cost_estimate=pl.CostEstimate(
            flops=60_000_000_000, bytes_accessed=20_000_000, transcendentals=4_000_000
        ),
        name="mix_backward",
    )(grad_rows, out_t, proj, tails, o, t, u, w, qe, a, s, wall, conv, dec, hg)


def matmul(left_side, right_side):
    return jnp.dot(left_side, right_side, preferred_element_type=f32)


def contract_rows(left_side, right_side):
    return lax.dot_general(
        left_side, right_side, (((0,), (0,)), ((), ())), preferred_element_type=f32
    )


def times_transposed(left_side, right_side):
    return lax.dot_general(
        left_side, right_side, (((1,), (1,)), ((), ())), preferred_element_type=f32
    )


def rms_scale(values, scale_gain):
    return (
        values
        * lax.rsqrt(jnp.mean(values * values, axis=-1, keepdims=True) + norm_eps)
        * scale_gain
    )


def group_rows(values):
    return lax.all_gather(values, "tensor", axis=0, tiled=True)


def row_sums(values):
    return lax.psum_scatter(
        values.astype(bf16), "tensor", scatter_dimension=0, tiled=True
    ).astype(f32)


def shards(
    block_input, out_cotangent, lengths, mixer_gain, query_weight, key_weight, value_weight,
    output_gate_weight, decay_weight, query_conv, key_conv, value_conv, decay_log, decay_bias,
    head_gain, out_weight, ffn_gain, ffn_gate, ffn_up, ffn_down,
):
    inputs = block_input.astype(f32)
    cotangent = out_cotangent.astype(f32)
    local_rows = inputs.shape[0]
    tensor_index = lax.axis_index("tensor")
    tensor_size = lax.axis_size("tensor")
    position = tensor_index * local_rows + jnp.arange(local_rows, dtype=jnp.int32)
    live_rows = (position < lengths[0]).astype(f32)[:, None]
    held = local_depth = query_weight.shape[0]
    decay_flat = decay_weight.reshape(local_depth, 2)
    mixer_pack = jnp.concatenate(
        [query_weight, key_weight, value_weight, output_gate_weight,
         jnp.pad(decay_flat, ((0, 0), (0, 126))), out_weight.T],
        axis=1,
    )
    ffn_pack = jnp.concatenate([ffn_gate, ffn_up, ffn_down.T], axis=1)
    normed_one, first_back = jax.vjp(rms_scale, inputs, mixer_gain)
    first_rows = group_rows(normed_one.astype(bf16))
    mixer_full = lax.all_gather(mixer_pack, "dp", axis=0, tiled=True)
    ffn_full = lax.all_gather(ffn_pack, "dp", axis=0, tiled=True)
    wall_back = mixer_full[:, :896]
    out_t = mixer_full[:, 896:]
    wall = jnp.concatenate(
        [mixer_full[:, :768],
         jnp.broadcast_to(mixer_full[:, 768:769], (D, DK)),
         jnp.broadcast_to(mixer_full[:, 769:770], (D, DK))],
        axis=1,
    )
    ff = ffn_gate.shape[1]
    ffn_in = ffn_full[:, : 2 * ff]
    down_t = ffn_full[:, 2 * ff :]
    conv = jnp.pad(
        jnp.concatenate([query_conv, key_conv, value_conv], axis=1), ((0, 4), (0, 0))
    )
    dec = jnp.pad(
        jnp.broadcast_to(jnp.stack([-jnp.exp(decay_log[0]), decay_bias[0]])[:, None], (2, DK)),
        ((0, 6), (0, 0)),
    )
    hg = head_gain[None, :]
    proj, mixed_part, mixed_rows, o, t, u, w, qe, a, s, tails = call_forward(
        first_rows, wall, conv, dec, hg, out_t
    )
    mixed = row_sums(mixed_part)
    middle = inputs + live_rows * mixed
    normed_two, second_back = jax.vjp(rms_scale, middle, ffn_gain)
    fed_grad = group_rows((live_rows * cotangent).astype(bf16))
    second_rows = group_rows(normed_two.astype(bf16))
    acts = matmul(second_rows, ffn_in)
    gate_act, up_act = acts[:, :ff], acts[:, ff:]
    sigmoid_gate = jax.nn.sigmoid(gate_act)
    hidden = (gate_act * sigmoid_gate * up_act).astype(bf16)
    hidden_grad = matmul(fed_grad, down_t)
    gate_grad = hidden_grad * up_act * sigmoid_gate * (1.0 + gate_act * (1.0 - sigmoid_gate))
    up_grad = hidden_grad * gate_act * sigmoid_gate
    act_grads = jnp.concatenate([gate_grad.astype(bf16), up_grad.astype(bf16)], axis=1)
    second_in = row_sums(times_transposed(act_grads, ffn_in))
    ffn_terms = row_sums(times_transposed(hidden, down_t))
    block_output = (middle + live_rows * ffn_terms).astype(bf16)
    acts_wgrad = contract_rows(second_rows, act_grads)
    down_wgrad = contract_rows(fed_grad, hidden)
    middle_part, ffn_gain_grad = second_back(second_in)
    middle_grad = cotangent + middle_part
    mixed_grad = group_rows((live_rows * middle_grad).astype(bf16))
    out_wgrad = contract_rows(mixed_grad, mixed_rows)
    early = jnp.concatenate(
        [acts_wgrad.astype(bf16), down_wgrad.astype(bf16), out_wgrad.astype(bf16)], axis=1
    )
    early_sum = lax.psum_scatter(early, "dp", scatter_dimension=0, tiled=True).astype(f32)
    pre_grads, first_part, conv_grads, small = call_backward(
        mixed_grad, out_t, (proj, o, t, u, w, qe, a, s, tails), wall_back, conv, dec, hg
    )
    first_sum = row_sums(first_part)
    late = contract_rows(first_rows, pre_grads).astype(bf16)
    late_sum = lax.psum_scatter(late, "dp", scatter_dimension=0, tiled=True).astype(f32)
    input_part, mixer_gain_grad = first_back(first_sum)
    input_grad = middle_grad + input_part
    own = jnp.concatenate(
        [conv_grads[:4].reshape(-1), small[1, :DK], small[2, :DK]]
    )
    slots = jnp.zeros((tensor_size, own.shape[0]), f32)
    slots = lax.dynamic_update_slice(slots, own[None, :], (tensor_index, 0))
    everything = lax.psum(
        jnp.concatenate([slots.reshape(-1), mixer_gain_grad, ffn_gain_grad, small[0]]),
        ("dp", "tensor"),
    )
    own_sum = lax.dynamic_slice(
        everything[: slots.size].reshape(slots.shape), (tensor_index, 0), (1, own.shape[0])
    )[0]
    gains = everything[slots.size :]
    conv_sum = own_sum[: 4 * QKV].reshape(4, QKV)
    return (
        block_output,
        input_grad,
        gains[:D],
        late_sum[:, :128],
        late_sum[:, 128:256],
        late_sum[:, 256:512],
        late_sum[:, 512:768],
        late_sum[:, 768:770].reshape(held, 1, 2),
        conv_sum[:, :DK],
        conv_sum[:, DK : 2 * DK],
        conv_sum[:, 2 * DK :],
        own_sum[4 * QKV : 4 * QKV + 1],
        own_sum[4 * QKV + DK : 4 * QKV + DK + 1],
        gains[2 * D :],
        early_sum[:, 3 * ff :].T,
        gains[D : 2 * D],
        early_sum[:, :ff],
        early_sum[:, ff : 2 * ff],
        early_sum[:, 2 * ff : 3 * ff].T,
    )


def solution(mesh):
    rows = P(("dp", "tensor"), None)
    tile = P("dp", "tensor")
    taps = P(None, "tensor")
    turned = P("tensor", "dp")
    decay = P("dp", "tensor", None)
    head = P("tensor")
    return jax.shard_map(
        shards,
        mesh=mesh,
        in_specs=(
            rows, rows, P("dp"), P(), tile, tile, tile, tile, decay, taps, taps, taps, head, head,
            P(), turned, P(), tile, tile, turned,
        ),
        out_specs=(
            rows, rows, P(), tile, tile, tile, tile, decay, taps, taps, taps, head, head,
            P(), turned, P(), tile, tile, turned,
        ),
        check_vma=False,
    )
```

time: 2170 us -> 863 us (0.40); the launches traced: 2140 us -> 862 us
  matrix products: 766 us -> 36.2 us
  blocking collectives: 408 us -> 0 us
  waiting for transfers between devices: 447 us -> 703 us
  other arithmetic: 269 us -> 19.5 us
  local copies, waits for them, and re-layouts: 223 us -> 33 us
  Pallas kernels: 0 us -> 52.7 us
    dot_general x1571 -> x2, matrix products: 697 us -> 13.8 us  [matmul(): return jnp.dot(left_side, right_side, preferred_element_type=f32)]
    all_gather x9 -> x0, blocking collectives: 294 us -> none  [the longest x1 54.7 us: shards(): lax.all_gather(ffn_gate, 'dp', axis=0, tiled=True)]
    reduce_scatter x12 -> x5, waiting for transfers between devices: 416 us -> 226 us  [the longest x4 174 us: row_sums(): lax.psum_scatter(values.astype(bf16), 'tensor', scatter_dimension=0, tile...]
    psum x0 -> x1, waiting for transfers between devices: none -> 145 us  [shards(): lax.psum(jnp.concatenate([slots.reshape(-1), mixer_gain_grad, ffn_gain_gr...]
    all_gather x4, waiting for transfers between devices: 30 us -> 160 us  [group_rows(): return lax.all_gather(values, 'tensor', axis=0, tiled=True)]
    psum x2 -> x0, blocking collectives: 113 us -> none  [the longest x1 75.7 us: shards(): lax.psum((mixer_gain_grad, ffn_gain_grad, head_gain_grad), ('dp', 'tensor'))]
    squeeze x120 -> x1, local copies, waits for them, and re-layouts: 109 us -> 0.77 us  [shards(): small[1, :DK]]
    all_gather x0 -> x2, waiting for transfers between devices: none -> 96.8 us  [the longest x1 50.5 us: shards(): ffn_full = lax.all_gather(ffn_pack, 'dp', axis=0, tiled=True)]
  transfers between devices with their start and end apart: 17 -> 13, of which waited for: 9 -> 13; matrix products, arithmetic and copies ran while one was open for 41% -> 6% of each run, Pallas kernels for 0% -> 0%
where the time goes in v1:
time: 863 us; the launch traced here: 862 us
  waiting for transfers between devices  703 us (81%)
  Pallas kernels  52.7 us (6%)
  matrix products  36.2 us (4%)
  local copies, waits for them, and re-layouts  33 us (4%)
  other arithmetic  19.5 us (2%)
  between operations  16.3 us (2%)
    reduce_scatter x4, waiting for transfers between devices, row_sums(): lax.psum_scatter(values.astype(bf16), 'tensor', scatter_dimension=0, tile...  174 us
    all_gather x4, waiting for transfers between devices, group_rows(): return lax.all_gather(values, 'tensor', axis=0, tiled=True)  160 us
    psum x1, waiting for transfers between devices, shards(): lax.psum(jnp.concatenate([slots.reshape(-1), mixer_gain_grad, ffn_gain_gr...  145 us
    unnamed x14, waiting for transfers between devices  75.2 us
    reduce_scatter x1, waiting for transfers between devices, shards(): lax.psum_scatter(late, 'dp', scatter_dimension=0, tiled=True).astype(f32)  52.3 us
    all_gather x1, waiting for transfers between devices, shards(): ffn_full = lax.all_gather(ffn_pack, 'dp', axis=0, tiled=True)  50.5 us
    all_gather x1, waiting for transfers between devices, shards(): mixer_full = lax.all_gather(mixer_pack, 'dp', axis=0, tiled=True)  46.3 us
    pallas_call x1, Pallas kernels, call_backward(): pl.pallas_call(mix_backward, grid=(steps,), in_specs=[tall(D), fixed((D,...  26.5 us
  transfers between devices with their start and end apart: 13, of which 13 were waited for; matrix products, arithmetic and copies ran while one was open for 6% of the time, Pallas kernels for 0%

profile of v1, /device:TPU:1, one launch (start us, length us, event | category | flops | bytes accessed | tf_op | source)
XLA Modules:
  0.0 861.7 jit_solution(4787175940147463780)
XLA Ops:
  7.2 0.8 copy.51
  8.0 0.7 constant_dynamic-update-slice_fusion.3
  8.7 0.7 constant_dynamic-update-slice_fusion.2
  9.4 0.8 constant_dynamic-update-slice_fusion.1
  10.2 0.8 constant_dynamic-update-slice_fusion
  11.0 0.8 bitcast_dynamic-update-slice_fusion
  11.7 0.7 copy-done.6
  12.5 1.2 fusion.13
  13.7 1.9 fusion.7
  17.0 1.3 select_maximum_fusion.conv_ref
  18.4 46.3 %all-gather.9.cloned.1.call-done = bf16[1024,1152]{1,0:T(8,128)(2,1)} async-done(((bf16[64,1152]{1,0:T(8,128)(2,1)}), bf16[1024,1152]{1,0:T(8,128)(2,1)}) %all-gather.9.cloned.1.call-update) | async-done | bytes 2359312 | tf_op jit(solution)/shard_map/all_gather | solution.py:459
  64.7 2.0 slice.155.out_ref
  67.4 0.7 slice-done
  68.1 1.6 pad_maximum_fusion.2.wall_ref
  69.8 37.0 %all-gather.7.cloned.1.call-done.first_ref = bf16[1536,1024]{1,0:T(8,128)(2,1)} async-done(((bf16[192,1024]{1,0:T(8,128)(2,1)}), bf16[1536,1024]{1,0:T(8,128)(2,1)}) %all-gather.7.cloned.1.call-update) | async-done | bytes 3145744 | tf_op jit(solution)/shard_map/all_gather | solution.py:428
  106.7 0.7 pad.17.dec_ref
  107.4 26.2 %mix_forward.1 = (f32[1536,1024]{1,0:T(8,128)}, bf16[1536,1024]{1,0:T(8,128)(2,1)}, bf16[1536,256]{1,0:T(8,128)(2,1)}, f32[1536,256]{1,0:T(8,128)}, bf16[6,256,2...) custom-call(bf16[1536,1024]{1,0:T(8,128)(2,1)} %all-gather.7.cloned., ...), custom_call_target="tpu_custom_call" | custom-call | flops 30000001024 | bytes 20000000 | tf_op jit(solution)/shard_map/mix_forward/pallas_call | solution.py:336
  133.8 0.7 copy-done.8
  134.5 0.8 concatenate.27
  136.0 42.5 %reduce-scatter.9.cloned.1.call-done = bf16[192,1024]{1,0:T(8,128)(2,1)} async-done(((bf16[1536,1024]{1,0:T(8,128)(2,1)}), bf16[192,1024]{1,0:T(8,128)(2,1)}) %reduce-scatter.9.cloned.1.call-update) | async-done | bytes 393232 | tf_op jit(solution)/shard_map/reduce_scatter | solution.py:432
  178.5 1.3 multiply_reduce_fusion
  179.8 2.1 fusion.9
  182.8 50.5 %all-gather.13.cloned.1.call-done = bf16[1024,1056]{1,0:T(8,128)(2,1)} async-done(((bf16[64,1056]{1,0:T(8,128)(2,1)}), bf16[1024,1056]{1,0:T(8,128)(2,1)}) %all-gather.13.cloned.1.call-update) | async-done | bytes 2162704 | tf_op jit(solution)/shard_map/all_gather | solution.py:460
  233.3 41.3 %all-gather.11.cloned.1.call-done = bf16[1536,1024]{1,0:T(8,128)(2,1)} async-done(((bf16[192,1024]{1,0:T(8,128)(2,1)}), bf16[1536,1024]{1,0:T(8,128)(2,1)}) %all-gather.11.cloned.1.call-update) | async-done | bytes 3145744 | tf_op jit(solution)/shard_map/all_gather | solution.py:428
  274.6 6.9 fusion.1
  281.5 38.5 %all-gather.15.cloned.1.call-done = bf16[1536,1024]{1,0:T(8,128)(2,1)} async-done(((bf16[192,1024]{1,0:T(8,128)(2,1)}), bf16[1536,1024]{1,0:T(8,128)(2,1)}) %all-gather.15.cloned.1.call-update) | async-done | bytes 3145744 | tf_op jit(solution)/shard_map/all_gather | solution.py:428
  320.0 6.9 multiply_convert_fusion.1
  326.9 1.0 copy-done.26
  328.4 4.2 convolution_convert_fusion
  332.6 44.6 %reduce-scatter.13.cloned.1.call-done = bf16[192,1024]{1,0:T(8,128)(2,1)} async-done(((bf16[1536,1024]{1,0:T(8,128)(2,1)}), bf16[192,1024]{1,0:T(8,128)(2,1)}) %reduce-scatter.13.cloned.1.call-update) | async-done | bytes 393232 | tf_op jit(solution)/shard_map/reduce_scatter | solution.py:432
  377.2 2.1 fusion.10
  379.3 0.7 multiply_multiply_fusion.1
  380.5 2.1 multiply_convert_fusion.3
  383.0 1.4 slice.160.wall_ref
  384.4 43.5 %all-gather.17.cloned.1.call-done.grad_ref = bf16[1536,1024]{1,0:T(8,128)(2,1)} async-done(((bf16[192,1024]{1,0:T(8,128)(2,1)}), bf16[1536,1024]{1,0:T(8,128)(2,1)}) %all-gather.17.cloned.1.call-update) | async-done | bytes 3145744 | tf_op jit(solution)/shard_map/all_gather | solution.py:428
  427.9 26.5 %mix_backward.1 = (bf16[1536,896]{1,0:T(8,128)(2,1)}, bf16[1536,1024]{1,0:T(8,128)(2,1)}, f32[8,512]{1,0:T(8,128)}, f32[8,256]{1,0:T(8,128)}) custom-call(bf16[1536,1024]{1,0:T(8,128)(2,1)} %all-gather.17.cloned.1.call-done.grad_ref, bf16[1024,256]{1,0:T(8,128)(2,1)} %slice.155.out_ref, f32[1536,1024]{1,0:T(8,128)} %get-tuple-element.35.proj_ref, ...), custom_call_target="tpu_custom_call" | custom-call | flops 60000002048 | bytes 20000000 | tf_op jit(solution)/shard_map/mix_backward/pallas_call | solution.py:376
  454.4 6.5 convolution_convert_fusion.2
  461.3 3.3 convolution_convert_fusion.4
  464.7 2.4 convolution_convert_fusion.3
  467.2 1.0 convolution_convert_fusion.5
  468.5 2.9 copy.57
  471.4 0.7 reduce-scatter.15.cloned.1.call-update
  472.6 5.0 convolution_convert_fusion.1
  477.7 0.7 slice.129
  478.4 0.8 slice_bitcast_fusion.4
  479.4 52.3 %reduce-scatter.17.cloned.1.call-done = bf16[64,896]{1,0:T(8,128)(2,1)} async-done(((bf16[1024,896]{1,0:T(8,128)(2,1)}), bf16[64,896]{1,0:T(8,128)(2,1)}) %reduce-scatter.17.cloned.1.call-update) | async-done | bytes 114704 | tf_op jit(solution)/shard_map/reduce_scatter | solution.py:514
  531.7 0.7 slice.166
  532.4 0.6 copy.52
  533.1 1.4 fusion.25
  534.4 1.4 fusion.24
  535.9 73.8 %reduce-scatter.19.cloned.1.call-done = bf16[64,1312]{1,0:T(8,128)(2,1)} async-done(((bf16[1024,1312]{1,0:T(8,128)(2,1)}), bf16[64,1312]{1,0:T(8,128)(2,1)}) %reduce-scatter.19.cloned.1.call-update) | async-done | bytes 167952
  609.7 1.1 copy.58
  610.9 0.8 copy.55
  611.7 0.8 copy.54
  612.4 0.8 copy.56
  613.2 0.7 copy.53
  613.9 40.5 %reduce-scatter.15.cloned.1.call-done = bf16[192,1024]{1,0:T(8,128)(2,1)} async-done(((bf16[1536,1024]{1,0:T(8,128)(2,1)}), bf16[192,1024]{1,0:T(8,128)(2,1)}) %reduce-scatter.15.cloned.1.call-update) | async-done | bytes 393232 | tf_op jit(solution)/shard_map/reduce_scatter | solution.py:432
  654.4 1.4 fusion.11
  656.4 46.2 %reduce-scatter.11.cloned.1.call-done = bf16[192,1024]{1,0:T(8,128)(2,1)} async-done(((bf16[1536,1024]{1,0:T(8,128)(2,1)}), bf16[192,1024]{1,0:T(8,128)(2,1)}) %reduce-scatter.11.cloned.1.call-update) | async-done | bytes 393232 | tf_op jit(solution)/shard_map/reduce_scatter | solution.py:432
  702.6 2.8 fusion.12
  705.4 144.6 %all-reduce.5.cloned.1.call-done = f32[20736]{0:T(1024)} async-done(((f32[20736]{0:T(1024)}), f32[20736]{0:T(1024)}) %all-reduce.5.cloned.1.call-update) | async-done | bytes 82960 | tf_op jit(solution)/shard_map/psum | solution.py:522
  850.0 0.9 slice.167
  852.7 1.2 slice.171
  853.9 1.3 fusion.26
  (111 shorter events, 7.5 us)
Async XLA Ops:
  7.2 57.5 %all-gather.9.cloned.1.call-start = ((), (), s32[]{:S(2)}) async-start(), calls=%async_computation.7 | async-start | bytes 2506752 | tf_op jit(solution)/shard_map/all_gather | solution.py:459
  11.7 0.7 copy-start.6
  12.4 94.3 %all-gather.7.cloned.1.call-start = ((), (), s32[]{:S(2)}) async-start(), calls=%async_computation.6 | async-start | bytes 3538944 | tf_op jit(solution)/shard_map/all_gather | solution.py:428
  13.6 53.1 %copy-start.15 = (f32[192]{0:T(256)}, f32[192]{0:T(256)S(1)}, u32[]{:S(2)}) copy-start(f32[192]{0:T(256)S(1)} %fusion.13) | copy-start | bytes 2308
  15.6 162.9 %reduce-scatter.9.cloned.1.call-start = ((), (), s32[]{:S(2)}) async-start(), calls=%async_computation.8 | async-start | bytes 3538944 | tf_op jit(solution)/shard_map/reduce_scatter | solution.py:432
  64.7 2.0 copy-start.2
  66.7 1.4 slice-start
  133.7 0.8 copy-start.8
  133.7 0.8 copy-start.9
  133.7 0.8 copy-start.10
  133.7 44.8 %copy-start = (bf16[192,1024]{1,0:T(8,128)(2,1)S(1)}, bf16[192,1024]{1,0:T(8,128)(2,1)}, u32[]{:S(2)}) copy-start(bf16[192,1024]{1,0:T(8,128)(2,1)} %param.20) | copy-start | bytes 1179652
  133.7 46.1 %copy-start.3 = (bf16[192,1024]{1,0:T(8,128)(2,1)S(1)}, bf16[192,1024]{1,0:T(8,128)(2,1)}, u32[]{:S(2)}) copy-start(bf16[192,1024]{1,0:T(8,128)(2,1)} %param.21) | copy-start | bytes 1179652
  133.7 46.1 %copy-start.7 = (f32[1024]{0:T(1024)S(1)}, f32[1024]{0:T(1024)}, u32[]{:S(2)}) copy-start(f32[1024]{0:T(1024)} %param.36) | copy-start | bytes 12292
  133.8 99.5 %all-gather.13.cloned.1.call-start = ((), (), s32[]{:S(2)}) async-start(), calls=%async_computation.10 | async-start | bytes 2506752 | tf_op jit(solution)/shard_map/all_gather | solution.py:460
  135.3 139.2 %all-gather.11.cloned.1.call-start = ((), (), s32[]{:S(2)}) async-start(), calls=%async_computation.9 | async-start | bytes 3538944 | tf_op jit(solution)/shard_map/all_gather | solution.py:428
  179.8 101.7 %copy-start.17 = (f32[192]{0:T(256)}, f32[192]{0:T(256)S(1)}, u32[]{:S(2)}) copy-start(f32[192]{0:T(256)S(1)} %multiply_reduce_fusion) | copy-start | bytes 2308
  181.9 138.1 %all-gather.15.cloned.1.call-start = ((), (), s32[]{:S(2)}) async-start(), calls=%async_computation.12 | async-start | bytes 3538944 | tf_op jit(solution)/shard_map/all_gather | solution.py:428
  182.5 194.7 %reduce-scatter.13.cloned.1.call-start = ((), (), s32[]{:S(2)}) async-start(), calls=%async_computation.13 | async-start | bytes 3538944 | tf_op jit(solution)/shard_map/reduce_scatter | solution.py:432
  320.0 8.4 copy-start.22
  326.9 1.0 copy-start.26
  326.9 1.5 copy-start.28
  332.5 44.7 %copy-start.1 = (bf16[192,1024]{1,0:T(8,128)(2,1)S(1)}, bf16[192,1024]{1,0:T(8,128)(2,1)}, u32[]{:S(2)}) copy-start(bf16[192,1024]{1,0:T(8,128)(2,1)} %reduce-scatter.9.cloned.1.call-done) | copy-start | bytes 1179652
  332.6 95.3 %all-gather.17.cloned.1.call-start = ((), (), s32[]{:S(2)}) async-start(), calls=%async_computation.14 | async-start | bytes 3538944 | tf_op jit(solution)/shard_map/all_gather | solution.py:428
  380.0 0.6 copy-start.13
  382.7 149.0 %reduce-scatter.17.cloned.1.call-start = ((), (), s32[]{:S(2)}) async-start(), calls=%async_computation.17 | async-start | bytes 1949696 | tf_op jit(solution)/shard_map/reduce_scatter | solution.py:514
  427.9 26.5 %copy-start.19 = (bf16[1536,1024]{1,0:T(8,128)(2,1)S(1)}, bf16[1536,1024]{1,0:T(8,128)(2,1)}, u32[]{:S(2)}) copy-start(bf16[1536,1024]{1,0:T(8,128)(2,1)} %all-gather.7.cloned.1.call-done.first_ref) | copy-start | bytes 9437188
  454.4 6.8 copy-start.24
  460.9 148.8 %reduce-scatter.19.cloned.1.call-start = ((), (), s32[]{:S(2)}) async-start(), calls=%async_computation.18 | async-start | bytes 3063808
  461.3 3.4 copy-start.20
  461.3 3.4 copy-start.27
  461.3 3.4 copy-start.29
  464.7 2.4 copy-start.21
  464.7 2.5 copy-start.23
  471.3 1.3 copy-start.25
  471.4 183.0 %reduce-scatter.15.cloned.1.call-start = ((), (), s32[]{:S(2)}) async-start(), calls=%async_computation.15 | async-start | bytes 3538944 | tf_op jit(solution)/shard_map/reduce_scatter | solution.py:432
  472.1 230.5 %reduce-scatter.11.cloned.1.call-start = ((), (), s32[]{:S(2)}) async-start(), calls=%async_computation.11 | async-start | bytes 3538944 | tf_op jit(solution)/shard_map/reduce_scatter | solution.py:432
  477.6 0.8 copy-start.18
  477.6 372.3 %all-reduce.5.cloned.1.call-start = ((), (), s32[]{:S(2)}) async-start(), calls=%async_computation.16 | async-start | bytes 172032 | tf_op jit(solution)/shard_map/psum | solution.py:522
  478.4 176.0 %copy-start.11 = (f32[1024]{0:T(1024)S(1)}, f32[1024]{0:T(1024)}, u32[]{:S(2)}) copy-start(f32[1024]{0:T(1024)} %param.23) | copy-start | bytes 12292
  535.9 119.9 %copy-start.16 = (f32[192]{0:T(256)S(1)}, f32[192]{0:T(256)}, u32[]{:S(2)}) copy-start(f32[192]{0:T(256)} %copy-done.15) | copy-start | bytes 2308
  535.9 119.9 %copy-start.12 = (f32[1024]{0:T(1024)S(1)}, f32[1024]{0:T(1024)}, u32[]{:S(2)}) copy-start(f32[1024]{0:T(1024)} %get-tuple-element.108) | copy-start | bytes 12292
  535.9 166.7 %copy-start.4 = (bf16[192,1024]{1,0:T(8,128)(2,1)S(1)}, bf16[192,1024]{1,0:T(8,128)(2,1)}, u32[]{:S(2)}) copy-start(bf16[192,1024]{1,0:T(8,128)(2,1)} %param.21) | copy-start | bytes 1179652
  535.9 166.7 %copy-start.5 = (bf16[192,1024]{1,0:T(8,128)(2,1)S(1)}, bf16[192,1024]{1,0:T(8,128)(2,1)}, u32[]{:S(2)}) copy-start(bf16[192,1024]{1,0:T(8,128)(2,1)} %reduce-scatter.13.cloned.1.call-done) | copy-start | bytes 1179652
  535.9 166.7 %copy-start.14 = (f32[192]{0:T(256)S(1)}, f32[192]{0:T(256)}, u32[]{:S(2)}) copy-start(f32[192]{0:T(256)} %copy-done.13) | copy-start | bytes 2308
Sparse Core Ops, SparseCore 0:
  12.6 52.0 all-gather.8
  66.9 39.7 all-gather.6
  133.9 44.5 reduce-scatter.8
  180.8 52.3 all-gather.12
  234.7 39.7 all-gather.10
  276.1 43.8 all-gather.14
  332.7 44.4 reduce-scatter.12
  382.8 45.0 all-gather.16
  461.1 70.6 reduce-scatter.16
  535.6 74.0 reduce-scatter.18
  612.2 42.1 reduce-scatter.14
  656.8 45.7 reduce-scatter.10
  708.0 141.8 all-reduce.4

commit v2 on v1

--- a/solution.py
+++ b/solution.py
@@ -11,6 +11,11 @@
 DV = 256
 QKV = 2 * DK + DV
 D = 1024
+GATE_END = 768
+PRE = 896
+MIX = 1152
+TENSOR = 8
+DATA = 16
 CHUNK = 256
 BATCH = 2
 
@@ -80,9 +85,11 @@
     return total
 
 
-def gates(decay_pre, write_pre, dec_ref):
-    z = decay_pre + dec_ref[1:2, :]
-    return z, dec_ref[0:1, :] * softplus(z), jax.nn.sigmoid(write_pre)
+def gates(proj_ref, rows, dec_ref):
+    both = proj_ref[rows, GATE_END:PRE]
+    z = jnp.broadcast_to(both[:, 0:1], (CHUNK, DK)) + dec_ref[1:2, :]
+    rate = jax.nn.sigmoid(jnp.broadcast_to(both[:, 1:2], (CHUNK, DK)))
+    return z, dec_ref[0:1, :] * softplus(z), rate
 
 
 def cumulative(decays, causal_ones):
@@ -97,7 +104,7 @@
 
 
 def mix_forward(
-    first_ref, wall_ref, conv_ref, dec_ref, hg_ref, out_ref,
+    first_ref, pack_ref, conv_ref, dec_ref, hg_ref,
     proj_ref, part_ref, mixed_ref, o_ref, t_ref, u_ref, w_ref, qe_ref, a_ref, s_ref, tail_ref,
     state, pad,
 ):
@@ -113,7 +120,7 @@
     parts = range(BATCH)
     rows = [pl.ds(c * CHUNK, CHUNK) for c in parts]
     for c in parts:
-        pre = mm(first_ref[rows[c], :], wall_ref[...])
+        pre = mm(first_ref[rows[c], :], pack_ref[:, :PRE])
         proj_ref[rows[c], :] = pre
         pad[pl.ds(8 + c * CHUNK, CHUNK), :] = pre[:, :QKV]
     items = []
@@ -123,9 +130,7 @@
         q, k, v = act[:, :DK], act[:, DK : 2 * DK], act[:, 2 * DK :]
         q = q * (lax.rsqrt(row_total(q * q) + norm_eps) * DK ** (-0.5))
         k = k * lax.rsqrt(row_total(k * k) + norm_eps)
-        _, decays, rate = gates(
-            proj_ref[rows[c], 768:896], proj_ref[rows[c], 896:1024], dec_ref
-        )
+        _, decays, rate = gates(proj_ref, rows[c], dec_ref)
         total, across = cumulative(decays, causal_ones)
         ratio = ratios(total, across, causal)
         kk = mm(k, k, 1, 1)
@@ -178,14 +183,14 @@
         o = mm(q_eff, starts[c], 1, 1) + mm(scores, u_start)
         o_ref[rows[c], :] = o
         normed = o * lax.rsqrt(row_total(o * o) * (1.0 / DV) + gate_eps) * hg_ref[...]
-        mixed = (normed * jax.nn.silu(proj_ref[rows[c], 512:768])).astype(bf16)
+        mixed = (normed * jax.nn.silu(proj_ref[rows[c], QKV:GATE_END])).astype(bf16)
         mixed_ref[rows[c], :] = mixed
-        part_ref[rows[c], :] = mm(mixed, out_ref[...], 1, 1).astype(bf16)
+        part_ref[rows[c], :] = mm(mixed, pack_ref[:, PRE:MIX], 1, 1).astype(bf16)
 
 
 def mix_backward(
-    grad_ref, out_ref, proj_ref, tail_ref, o_ref, t_ref, u_ref, w_ref, qe_ref, a_ref, s_ref,
-    wall_ref, conv_ref, dec_ref, hg_ref,
+    grad_ref, pack_ref, proj_ref, tail_ref, o_ref, t_ref, u_ref, w_ref, qe_ref, a_ref, s_ref,
+    conv_ref, dec_ref, hg_ref,
     pre_ref, first_ref, conv_grad_ref, small_ref,
     dstate, padp, padg,
 ):
@@ -219,9 +224,7 @@
         k_scale = lax.rsqrt(row_total(kc * kc) + norm_eps)
         q = qc * (q_scale * DK ** (-0.5))
         k = kc * k_scale
-        z, decays, rate = gates(
-            proj_ref[rows[c], 768:896], proj_ref[rows[c], 896:1024], dec_ref
-        )
+        z, decays, rate = gates(proj_ref, rows[c], dec_ref)
         total, across = cumulative(decays, causal_ones)
         ratio = ratios(total, across, causal)
         key_ratio = mm(k, k, 1, 1) * ratio
@@ -229,8 +232,8 @@
         growth = jnp.exp(total)
         last = total[CHUNK - 1 : CHUNK, :]
         tail = jnp.exp(last - total)
-        grad = mm(grad_ref[rows[c], :], out_ref[...])
-        gate = proj_ref[rows[c], 512:768]
+        grad = mm(grad_ref[rows[c], :], pack_ref[:, PRE:MIX])
+        gate = proj_ref[rows[c], QKV:GATE_END]
         gate_sig = jax.nn.sigmoid(gate)
         gate_act = gate * gate_sig
         o = o_ref[rows[c], :]
@@ -238,7 +241,7 @@
         normed = o * o_scale
         gain = hg_ref[...]
         gate_grad = grad * normed * gain * gate_sig * (1.0 + gate * (1.0 - gate_sig))
-        pre_ref[rows[c], 512:768] = gate_grad.astype(bf16)
+        pre_ref[rows[c], QKV:GATE_END] = gate_grad.astype(bf16)
         grad = grad * gate_act
         small_ref[0:1, :] += jnp.sum(grad * normed, axis=0, keepdims=True)
         grad = grad * gain
@@ -303,7 +306,7 @@
         )
         dz = d_decay * dec_ref[0:1, :] * jax.nn.sigmoid(z)
         d_write = d_rate * rate * (1.0 - rate)
-        pre_ref[rows[c], 768:896] = jnp.where(
+        pre_ref[rows[c], GATE_END:PRE] = jnp.where(
             lane == 0, dz, jnp.where(lane == 1, d_write, 0.0)
         ).astype(bf16)
         small_ref[1:2, :DK] += jnp.sum(d_decay * decays, axis=0, keepdims=True)
@@ -321,11 +324,11 @@
                 dact * padp[pl.ds(c * CHUNK + 5 + tap, CHUNK), :], axis=0, keepdims=True
             )
         pre_ref[rows[c], :QKV] = dpre.astype(bf16)
-        first_ref[rows[c], :] = mm(pre_ref[rows[c], :], wall_ref[...], 1, 1).astype(bf16)
+        first_ref[rows[c], :] = mm(pre_ref[rows[c], :], pack_ref[:, :PRE], 1, 1).astype(bf16)
     padg[pl.ds(BATCH * CHUNK, 8), :] = padg[0:8, :]
 
 
-def call_forward(first_rows, wall, conv, dec, hg, out_t):
+def call_forward(first_rows, pack, conv, dec, hg):
     rows = first_rows.shape[0]
     chunks = rows // CHUNK
     steps = chunks // BATCH
@@ -337,15 +340,14 @@
         mix_forward,
         grid=(steps,),
         in_specs=[
-            tall(D), fixed((D, 1024)), fixed((8, QKV)), fixed((8, DK)), fixed((1, DV)),
-            fixed((D, DV)),
+            tall(D), fixed((D, MIX)), fixed((8, QKV)), fixed((8, DK)), fixed((1, DV)),
         ],
         out_specs=[
-            tall(1024), tall(D), tall(DV), tall(DV), per(CHUNK, CHUNK), per(CHUNK, DV),
+            tall(PRE), tall(D), tall(DV), tall(DV), per(CHUNK, CHUNK), per(CHUNK, DV),
             per(CHUNK, DK), per(CHUNK, DK), per(DK, DK), per(DV, DK), per(8, QKV),
         ],
         out_shape=[
-            made((rows, 1024), f32), made((rows, D), bf16), made((rows, DV), bf16),
+            made((rows, PRE), f32), made((rows, D), bf16), made((rows, DV), bf16),
             made((rows, DV), f32), made((chunks, CHUNK, CHUNK), bf16),
             made((chunks, CHUNK, DV), bf16), made((chunks, CHUNK, DK), bf16),
             made((chunks, CHUNK, DK), bf16), made((chunks, DK, DK), f32),
@@ -361,10 +363,10 @@
             flops=30_000_000_000, bytes_accessed=20_000_000, transcendentals=4_000_000
         ),
         name="mix_forward",
-    )(first_rows, wall, conv, dec, hg, out_t)
-
-
-def call_backward(grad_rows, out_t, saved, wall, conv, dec, hg):
+    )(first_rows, pack, conv, dec, hg)
+
+
+def call_backward(grad_rows, pack, saved, conv, dec, hg):
     proj, o, t, u, w, qe, a, s, tails = saved
     rows = grad_rows.shape[0]
     chunks = rows // CHUNK
@@ -377,13 +379,13 @@
         mix_backward,
         grid=(steps,),
         in_specs=[
-            tall(D), fixed((D, DV)), tall(1024), per(8, QKV), tall(DV), per(CHUNK, CHUNK),
+            tall(D), fixed((D, MIX)), tall(PRE), per(8, QKV), tall(DV), per(CHUNK, CHUNK),
             per(CHUNK, DV), per(CHUNK, DK), per(CHUNK, DK), per(DK, DK), per(DV, DK),
-            fixed((D, 896)), fixed((8, QKV)), fixed((8, DK)), fixed((1, DV)),
+            fixed((8, QKV)), fixed((8, DK)), fixed((1, DV)),
         ],
-        out_specs=[tall(896), tall(D), fixed((8, QKV)), fixed((8, DV))],
+        out_specs=[tall(PRE), tall(D), fixed((8, QKV)), fixed((8, DV))],
         out_shape=[
-            made((rows, 896), bf16), made((rows, D), bf16), made((8, QKV), f32),
+            made((rows, PRE), bf16), made((rows, D), bf16), made((8, QKV), f32),
             made((8, DV), f32),
         ],
         scratch_shapes=[
@@ -397,7 +399,463 @@
             flops=60_000_000_000, bytes_accessed=20_000_000, transcendentals=4_000_000
         ),
         name="mix_backward",
-    )(grad_rows, out_t, proj, tails, o, t, u, w, qe, a, s, wall, conv, dec, hg)
+    )(grad_rows, pack, proj, tails, o, t, u, w, qe, a, s, conv, dec, hg)
+
+
+class Wires:
+    def __init__(self, send, recv):
+        self.send, self.recv, self.sent = send, recv, []
+
+    def put(self, source, target, device):
+        k = len(self.sent)
+        copy = pltpu.make_async_remote_copy(
+            src_ref=source,
+            dst_ref=target,
+            send_sem=self.send.at[k],
+            recv_sem=self.recv.at[k],
+            device_id=device,
+            device_id_type=pl.DeviceIdType.MESH,
+        )
+        copy.start()
+        self.sent.append(copy)
+        return copy
+
+    def flush(self):
+        for copy in self.sent:
+            copy.wait_send()
+
+
+def on_tensor(index):
+    return {"tensor": index}
+
+
+def on_data(index):
+    return {"dp": index}
+
+
+def tensor_places():
+    me = lax.axis_index("tensor")
+    x, y = me % 4, me // 4
+    at = lambda side, step: side * 4 + (x + step) % 4
+    return {
+        "me": at(y, 0), "right": at(y, 1), "far": at(y, 2), "left": at(y, 3),
+        "mate": at(1 - y, 0), "mate_right": at(1 - y, 1), "mate_far": at(1 - y, 2),
+        "mate_left": at(1 - y, 3),
+    }
+
+
+def data_places():
+    me = lax.axis_index("dp")
+    core, z, y = me % 2, (me // 2) % 4, me // 8
+    at = lambda side, step, unit: (side * 4 + (z + step) % 4) * 2 + unit
+    here = {
+        "me": at(y, 0, core), "up": at(y, 1, core), "far": at(y, 2, core),
+        "down": at(y, 3, core), "over": at(1 - y, 0, core), "over_up": at(1 - y, 1, core),
+        "over_far": at(1 - y, 2, core), "over_down": at(1 - y, 3, core),
+    }
+    core_mate = {name: at(1 - y if "over" in name else y, step, 1 - core)
+                 for name, step in (("me", 0), ("up", 1), ("far", 2), ("down", 3), ("over", 0),
+                                    ("over_up", 1), ("over_far", 2), ("over_down", 3))}
+    return here, core_mate
+
+
+def greet(devices):
+    barrier = pltpu.get_barrier_semaphore()
+    for device in devices:
+        pl.semaphore_signal(
+            barrier, inc=1, device_id=device, device_id_type=pl.DeviceIdType.MESH
+        )
+    pl.semaphore_wait(barrier, len(devices))
+
+
+def together(*steps):
+    running = list(steps)
+    while running:
+        for item in list(running):
+            try:
+                next(item)
+            except StopIteration:
+                running.remove(item)
+
+
+def block(ref, index, size, start=0, length=None):
+    return ref.at[pl.ds(pl.multiple_of(index * size + start, 16), length or size)]
+
+
+def gather_tensor(wires, place, own, out):
+    size = own.shape[0]
+    half = size // 2
+    at = lambda who, part: block(out, place[who], size, part * half, half)
+    send = lambda who, part, to: wires.put(at(who, part), at(who, part), on_tensor(place[to]))
+    first = {}
+    for part in (0, 1):
+        for to in ("mate", "right", "left"):
+            first[to, part] = wires.put(
+                own.at[pl.ds(part * half, half)], at("me", part), on_tensor(place[to])
+            )
+    yield
+    first["left", 0].wait_recv()
+    far_low = send("right", 0, "left")
+    yield
+    first["mate", 0].wait_recv()
+    second = [send("mate", 0, "right"), send("mate", 0, "left")]
+    yield
+    first["right", 0].wait_recv()
+    first["right", 1].wait_recv()
+    far_high = send("left", 1, "right")
+    yield
+    far_low.wait_recv()
+    second.append(send("far", 0, "mate"))
+    yield
+    first["left", 1].wait_recv()
+    first["mate", 1].wait_recv()
+    second += [send("mate", 1, "right"), send("mate", 1, "left")]
+    yield
+    far_high.wait_recv()
+    second.append(send("far", 1, "mate"))
+    yield
+    for copy in second:
+        copy.wait_recv()
+
+
+GATHER_TENSOR = 14
+
+
+def gather_data(wires, place, core_mate, own, out):
+    size = own.shape[0]
+    half = size // 2
+    at = lambda who: block(out, place[who], size)
+    part = lambda who, i: block(out, place[who], size, i * half, half)
+    send = lambda ref, to: wires.put(ref, ref, on_data(place[to]))
+    share = lambda ref: wires.put(ref, ref, on_data(core_mate["me"]))
+    first = {to: wires.put(own, at("me"), on_data(place[to])) for to in ("over", "up", "down")}
+    shared = [wires.put(own, at("me"), on_data(core_mate["me"]))]
+    yield
+    first["up"].wait_recv()
+    far_high = send(part("down", 1), "up")
+    shared.append(share(at("down")))
+    yield
+    first["down"].wait_recv()
+    far_low = send(part("up", 0), "down")
+    shared.append(share(at("up")))
+    yield
+    first["over"].wait_recv()
+    second = {to: send(at("over"), to) for to in ("up", "down")}
+    shared.append(share(at("over")))
+    yield
+    far_high.wait_recv()
+    shared.append(share(part("far", 1)))
+    far_low.wait_recv()
+    shared.append(share(part("far", 0)))
+    yield
+    second["up"].wait_recv()
+    far_high = send(part("over_down", 1), "up")
+    shared.append(share(at("over_down")))
+    yield
+    second["down"].wait_recv()
+    far_low = send(part("over_up", 0), "down")
+    shared.append(share(at("over_up")))
+    yield
+    far_high.wait_recv()
+    shared.append(share(part("over_far", 1)))
+    far_low.wait_recv()
+    shared.append(share(part("over_far", 0)))
+    yield
+    for copy in shared:
+        copy.wait_recv()
+
+
+GATHER_DATA = 19
+
+
+def scatter_tensor(wires, place, part_ref, slots, done):
+    size = part_ref.shape[0] // TENSOR
+    half = size // 2
+    rows = lambda who, start=0, length=None: block(part_ref, place[who], size, start, length)
+    load = lambda ref: ref[...].astype(f32)
+    slot = lambda i: slots.at[i]
+    piece = lambda i, p: slots.at[i, pl.ds(p * half, half)]
+    put = lambda source, target, to: wires.put(source, target, on_tensor(place[to]))
+    far = put(rows("mate_far"), slot(0), "mate")
+    to_right = put(rows("mate_right"), slot(1), "right")
+    to_left = put(rows("mate_left"), slot(2), "left")
+    yield
+    far.wait_recv()
+    slot(3)[...] = (load(slot(0)) + load(rows("far"))).astype(bf16)
+    pass_right = put(piece(3, 1), piece(4, 1), "right")
+    pass_left = put(piece(3, 0), piece(4, 0), "left")
+    near = [
+        put(rows("right", 0, half), piece(5, 0), "right"),
+        put(rows("left", half, half), piece(6, 1), "left"),
+    ]
+    yield
+    to_right.wait_recv()
+    to_left.wait_recv()
+    slot(7)[...] = (load(slot(1)) + load(slot(2)) + load(rows("mate"))).astype(bf16)
+    mate = put(slot(7), slot(8), "mate")
+    yield
+    pass_right.wait_recv()
+    piece(9, 1)[...] = (load(piece(4, 1)) + load(rows("right", half, half))).astype(bf16)
+    near.append(put(piece(9, 1), piece(5, 1), "right"))
+    pass_left.wait_recv()
+    piece(9, 0)[...] = (load(piece(4, 0)) + load(rows("left", 0, half))).astype(bf16)
+    near.append(put(piece(9, 0), piece(6, 0), "left"))
+    yield
+    mate.wait_recv()
+    for copy in near:
+        copy.wait_recv()
+    done(load(rows("me")) + load(slot(5)) + load(slot(6)) + load(slot(8)))
+
+
+SCATTER_TENSOR = 10
+SCATTER_SLOTS = 10
+NAMES = ("far", "over_far", "up", "over_up", "down", "over_down", "me", "over")
+
+
+def scatter_data(wires, place, core_mate, part_ref, given, added, slots, out_ref):
+    size = part_ref.shape[0] // DATA
+    half = size // 2
+    load = lambda ref: ref[...].astype(f32)
+    number = {name: i for i, name in enumerate(NAMES)}
+    mine = lambda name: added.at[number[name]]
+    mine_part = lambda name, p: added.at[number[name], pl.ds(p * half, half)]
+    slot = lambda i: slots.at[i]
+    piece = lambda i, p: slots.at[i, pl.ds(p * half, half)]
+    put = lambda source, target, to: wires.put(source, target, on_data(place[to]))
+    swaps = [
+        wires.put(
+            block(part_ref, core_mate[name], size), given.at[i], on_data(core_mate["me"])
+        )
+        for i, name in enumerate(NAMES)
+    ]
+
+    def add_up(name):
+        i = number[name]
+        swaps[i].wait_recv()
+        mine(name)[...] = (load(given.at[i]) + load(block(part_ref, place[name], size))).astype(
+            bf16
+        )
+
+    yield
+    passed, near = [], []
+    for i, side in enumerate(("", "over_")):
+        add_up(side + "far")
+        passed.append(
+            (
+                put(mine_part(side + "far", 1), piece(i, 1), "up"),
+                put(mine_part(side + "far", 0), piece(i, 0), "down"),
+            )
+        )
+    yield
+    for i, side in enumerate(("", "over_")):
+        add_up(side + "up")
+        near.append(put(mine_part(side + "up", 0), piece(2 + i, 0), "up"))
+        add_up(side + "down")
+        near.append(put(mine_part(side + "down", 1), piece(4 + i, 1), "down"))
+    add_up("me")
+    add_up("over")
+    yield
+    for i, side in enumerate(("", "over_")):
+        up, down = passed[i]
+        up.wait_recv()
+        target = mine_part(side + "up", 1)
+        target[...] = (load(target) + load(piece(i, 1))).astype(bf16)
+        near.append(put(target, piece(2 + i, 1), "up"))
+        down.wait_recv()
+        target = mine_part(side + "down", 0)
+        target[...] = (load(target) + load(piece(i, 0))).astype(bf16)
+        near.append(put(target, piece(4 + i, 0), "down"))
+        yield
+    for copy in near:
+        copy.wait_recv()
+    slot(6)[...] = (load(mine("over")) + load(slot(3)) + load(slot(5))).astype(bf16)
+    last = put(slot(6), slot(7), "over")
+    out_ref[...] = load(mine("me")) + load(slot(2)) + load(slot(4))
+    yield
+    last.wait_recv()
+    out_ref[...] += load(slot(7))
+
+
+SCATTER_DATA = 21
+
+
+def rms_rows(values):
+    return lax.rsqrt(row_total(values * values) * (1.0 / D) + norm_eps)
+
+
+def rms_back(values, scale, gain, grad):
+    shared = grad * gain
+    inner = row_total(shared * values) * (1.0 / D)
+    return scale * shared - values * (scale * scale * scale * inner)
+
+
+TENSOR_NEAR = ("right", "left", "mate")
+DATA_NEAR = ("over", "up", "down")
+
+
+def start_kernel(
+    x_ref, gain_ref, pack_ref, first_ref, full_ref, own, send, recv, local,
+):
+    place = tensor_places()
+    data_place, core_mate = data_places()
+    x = x_ref[...].astype(f32)
+    own[...] = (x * rms_rows(x) * gain_ref[...]).astype(bf16)
+    greet(
+        [on_tensor(place[to]) for to in TENSOR_NEAR]
+        + [on_data(data_place[to]) for to in DATA_NEAR]
+        + [on_data(core_mate["me"])]
+    )
+    keep = [
+        pltpu.make_async_copy(own, block(first_ref, place["me"], own.shape[0]), local.at[0]),
+        pltpu.make_async_copy(
+            pack_ref, block(full_ref, data_place["me"], pack_ref.shape[0]), local.at[1]
+        ),
+    ]
+    for copy in keep:
+        copy.start()
+    wires = Wires(send, recv)
+    together(
+        gather_tensor(wires, place, own, first_ref),
+        gather_data(wires, data_place, core_mate, pack_ref, full_ref),
+    )
+    wires.flush()
+    for copy in keep:
+        copy.wait()
+
+
+def middle_kernel(
+    part_ref, x_ref, live_ref, gain_ref, middle_ref, second_ref, slots, own, send, recv, local,
+):
+    place = tensor_places()
+    greet([on_tensor(place[to]) for to in TENSOR_NEAR])
+    wires = Wires(send, recv)
+
+    def done(mixed):
+        middle = x_ref[...].astype(f32) + live_ref[...] * mixed
+        middle_ref[...] = middle
+        own[...] = (middle * rms_rows(middle) * gain_ref[...]).astype(bf16)
+
+    together(scatter_tensor(wires, place, part_ref, slots, done))
+    keep = pltpu.make_async_copy(own, block(second_ref, place["me"], own.shape[0]), local.at[0])
+    keep.start()
+    together(gather_tensor(wires, place, own, second_ref))
+    wires.flush()
+    keep.wait()
+
+
+def turn_kernel(
+    part_ref, middle_ref, cot_ref, live_ref, gain_ref, grad_ref, mixed_ref, gain_grad_ref,
+    slots, own, send, recv, local,
+):
+    place = tensor_places()
+    greet([on_tensor(place[to]) for to in TENSOR_NEAR])
+    wires = Wires(send, recv)
+
+    def done(second_in):
+        middle = middle_ref[...]
+        scale = rms_rows(middle)
+        gain_grad_ref[...] = jnp.sum(second_in * middle * scale, axis=0, keepdims=True)
+        grad = cot_ref[...].astype(f32) + rms_back(middle, scale, gain_ref[...], second_in)
+        grad_ref[...] = grad
+        own[...] = (live_ref[...] * grad).astype(bf16)
+
+    together(scatter_tensor(wires, place, part_ref, slots, done))
+    keep = pltpu.make_async_copy(own, block(mixed_ref, place["me"], own.shape[0]), local.at[0])
+    keep.start()
+    together(gather_tensor(wires, place, own, mixed_ref))
+    wires.flush()
+    keep.wait()
+
+
+def end_kernel(
+    part_ref, weight_ref, x_ref, grad_ref, gain_ref, gains_ref, head_ref,
+    input_ref, weight_out, gains_out, head_out,
+    slots, given, added, data_slots, gain_own, gain_slots, wide_own, wide_slots, head_slots,
+    send, recv,
+):
+    place = tensor_places()
+    data_place, core_mate = data_places()
+    me, data_me = place["me"], data_place["me"]
+    others = [lax.rem(me + i, TENSOR) for i in range(1, TENSOR)]
+    data_others = [lax.rem(data_me + i, DATA) for i in range(1, DATA)]
+    greet([on_tensor(i) for i in others] + [on_data(i) for i in data_others])
+    wires = Wires(send, recv)
+
+    def done(first_in):
+        x = x_ref[...].astype(f32)
+        scale = rms_rows(x)
+        gain_own[...] = gains_ref[...]
+        gain_own[0:1, :] = jnp.sum(first_in * x * scale, axis=0, keepdims=True)
+        input_ref[...] = grad_ref[...] + rms_back(x, scale, gain_ref[...], first_in)
+
+    def gains():
+        heads = [
+            wires.put(head_ref, head_slots.at[i], on_data(to))
+            for i, to in enumerate(data_others)
+        ]
+        yield
+        yield
+        yield
+        yield from scatter_tensor(wires, place, part_ref, slots, done)
+        near = [
+            wires.put(gain_own, gain_slots.at[i], on_tensor(to))
+            for i, to in enumerate(others)
+        ]
+        for copy in near:
+            copy.wait_recv()
+        total = gain_own[...]
+        for i in range(TENSOR - 1):
+            total = total + gain_slots[i]
+        wide_own[...] = total
+        all_data = [
+            wires.put(wide_own, wide_slots.at[i], on_data(to))
+            for i, to in enumerate(data_others)
+        ]
+        yield
+        for copy in heads:
+            copy.wait_recv()
+        total = head_ref[...]
+        for i in range(DATA - 1):
+            total = total + head_slots[i]
+        head_out[...] = total
+        yield
+        for copy in all_data:
+            copy.wait_recv()
+        total = wide_own[...]
+        for i in range(DATA - 1):
+            total = total + wide_slots[i]
+        gains_out[...] = total
+
+    together(
+        scatter_data(
+            wires, data_place, core_mate, weight_ref, given, added, data_slots, weight_out
+        ),
+        gains(),
+    )
+    wires.flush()
+
+
+END_COPIES = SCATTER_TENSOR + SCATTER_DATA + TENSOR - 1 + 2 * (DATA - 1)
+
+
+def communicate(kernel, number, outs, in_any, scratch, copies, operands, name):
+    vmem = pl.BlockSpec(memory_space=pltpu.VMEM)
+    return pl.pallas_call(
+        kernel,
+        out_shape=[jax.ShapeDtypeStruct(shape, kind) for shape, kind, _ in outs],
+        in_specs=[vmem] * len(operands),
+        out_specs=[pl.BlockSpec(memory_space=pl.ANY) if far else vmem for _, _, far in outs],
+        scratch_shapes=scratch
+        + [pltpu.SemaphoreType.DMA((copies,)), pltpu.SemaphoreType.DMA((copies,))]
+        + ([pltpu.SemaphoreType.DMA((2,))] if in_any else []),
+        compiler_params=pltpu.CompilerParams(
+            collective_id=number, has_side_effects=True, vmem_limit_bytes=56 * 1024 * 1024
+        ),
+        cost_estimate=pl.CostEstimate(
+            flops=30_000_000_000, bytes_accessed=20_000_000, transcendentals=0
+        ),
+        name=name,
+    )(*operands)
 
 
 def matmul(left_side, right_side):
@@ -413,14 +871,6 @@
 def times_transposed(left_side, right_side):
     return lax.dot_general(
         left_side, right_side, (((1,), (1,)), ((), ())), preferred_element_type=f32
-    )
-
-
-def rms_scale(values, scale_gain):
-    return (
-        values
-        * lax.rsqrt(jnp.mean(values * values, axis=-1, keepdims=True) + norm_eps)
-        * scale_gain
     )
 
 
@@ -439,36 +889,19 @@
     output_gate_weight, decay_weight, query_conv, key_conv, value_conv, decay_log, decay_bias,
     head_gain, out_weight, ffn_gain, ffn_gate, ffn_up, ffn_down,
 ):
-    inputs = block_input.astype(f32)
-    cotangent = out_cotangent.astype(f32)
-    local_rows = inputs.shape[0]
-    tensor_index = lax.axis_index("tensor")
-    tensor_size = lax.axis_size("tensor")
-    position = tensor_index * local_rows + jnp.arange(local_rows, dtype=jnp.int32)
-    live_rows = (position < lengths[0]).astype(f32)[:, None]
-    held = local_depth = query_weight.shape[0]
-    decay_flat = decay_weight.reshape(local_depth, 2)
-    mixer_pack = jnp.concatenate(
+    local_rows = block_input.shape[0]
+    rows = local_rows * TENSOR
+    depth = query_weight.shape[0]
+    ff = ffn_gate.shape[1]
+    width = MIX + 3 * ff
+    position = lax.axis_index("tensor") * local_rows + jnp.arange(local_rows, dtype=jnp.int32)
+    live = (position < lengths[0]).astype(f32)[:, None]
+    pack = jnp.concatenate(
         [query_weight, key_weight, value_weight, output_gate_weight,
-         jnp.pad(decay_flat, ((0, 0), (0, 126))), out_weight.T],
+         jnp.pad(decay_weight.reshape(depth, 2), ((0, 0), (0, 126))), out_weight.T,
+         ffn_gate, ffn_up, ffn_down.T],
         axis=1,
     )
-    ffn_pack = jnp.concatenate([ffn_gate, ffn_up, ffn_down.T], axis=1)
-    normed_one, first_back = jax.vjp(rms_scale, inputs, mixer_gain)
-    first_rows = group_rows(normed_one.astype(bf16))
-    mixer_full = lax.all_gather(mixer_pack, "dp", axis=0, tiled=True)
-    ffn_full = lax.all_gather(ffn_pack, "dp", axis=0, tiled=True)
-    wall_back = mixer_full[:, :896]
-    out_t = mixer_full[:, 896:]
-    wall = jnp.concatenate(
-        [mixer_full[:, :768],
-         jnp.broadcast_to(mixer_full[:, 768:769], (D, DK)),
-         jnp.broadcast_to(mixer_full[:, 769:770], (D, DK))],
-        axis=1,
-    )
-    ff = ffn_gate.shape[1]
-    ffn_in = ffn_full[:, : 2 * ff]
-    down_t = ffn_full[:, 2 * ff :]
     conv = jnp.pad(
         jnp.concatenate([query_conv, key_conv, value_conv], axis=1), ((0, 4), (0, 0))
     )
@@ -477,14 +910,24 @@
         ((0, 6), (0, 0)),
     )
     hg = head_gain[None, :]
+    local_block = pltpu.VMEM((local_rows, D), bf16)
+    scatter_slots = pltpu.VMEM((SCATTER_SLOTS, local_rows, D), bf16)
+    first_rows, full = communicate(
+        start_kernel, 1, [((rows, D), bf16, True), ((D, width), bf16, True)], True,
+        [local_block], GATHER_TENSOR + GATHER_DATA,
+        (block_input, mixer_gain[None, :], pack), "start_gathers",
+    )
+    fed_grad = group_rows((live * out_cotangent.astype(f32)).astype(bf16))
+    ffn_in = full[:, MIX : MIX + 2 * ff]
+    down_t = full[:, MIX + 2 * ff :]
     proj, mixed_part, mixed_rows, o, t, u, w, qe, a, s, tails = call_forward(
-        first_rows, wall, conv, dec, hg, out_t
-    )
-    mixed = row_sums(mixed_part)
-    middle = inputs + live_rows * mixed
-    normed_two, second_back = jax.vjp(rms_scale, middle, ffn_gain)
-    fed_grad = group_rows((live_rows * cotangent).astype(bf16))
-    second_rows = group_rows(normed_two.astype(bf16))
+        first_rows, full, conv, dec, hg
+    )
+    middle, second_rows = communicate(
+        middle_kernel, 2, [((local_rows, D), f32, False), ((rows, D), bf16, True)], True,
+        [scatter_slots, local_block], GATHER_TENSOR + SCATTER_TENSOR,
+        (mixed_part, block_input, live, ffn_gain[None, :]), "middle_sums",
+    )
     acts = matmul(second_rows, ffn_in)
     gate_act, up_act = acts[:, :ff], acts[:, ff:]
     sigmoid_gate = jax.nn.sigmoid(gate_act)
@@ -493,61 +936,68 @@
     gate_grad = hidden_grad * up_act * sigmoid_gate * (1.0 + gate_act * (1.0 - sigmoid_gate))
     up_grad = hidden_grad * gate_act * sigmoid_gate
     act_grads = jnp.concatenate([gate_grad.astype(bf16), up_grad.astype(bf16)], axis=1)
-    second_in = row_sums(times_transposed(act_grads, ffn_in))
+    second_part = times_transposed(act_grads, ffn_in).astype(bf16)
+    middle_grad, mixed_grad, ffn_gain_grad = communicate(
+        turn_kernel, 3,
+        [((local_rows, D), f32, False), ((rows, D), bf16, True), ((1, D), f32, False)], True,
+        [scatter_slots, local_block], GATHER_TENSOR + SCATTER_TENSOR,
+        (second_part, middle, out_cotangent, live, ffn_gain[None, :]), "turn_sums",
+    )
     ffn_terms = row_sums(times_transposed(hidden, down_t))
-    block_output = (middle + live_rows * ffn_terms).astype(bf16)
+    block_output = (middle + live * ffn_terms).astype(bf16)
     acts_wgrad = contract_rows(second_rows, act_grads)
     down_wgrad = contract_rows(fed_grad, hidden)
-    middle_part, ffn_gain_grad = second_back(second_in)
-    middle_grad = cotangent + middle_part
-    mixed_grad = group_rows((live_rows * middle_grad).astype(bf16))
     out_wgrad = contract_rows(mixed_grad, mixed_rows)
-    early = jnp.concatenate(
-        [acts_wgrad.astype(bf16), down_wgrad.astype(bf16), out_wgrad.astype(bf16)], axis=1
-    )
-    early_sum = lax.psum_scatter(early, "dp", scatter_dimension=0, tiled=True).astype(f32)
     pre_grads, first_part, conv_grads, small = call_backward(
-        mixed_grad, out_t, (proj, o, t, u, w, qe, a, s, tails), wall_back, conv, dec, hg
-    )
-    first_sum = row_sums(first_part)
-    late = contract_rows(first_rows, pre_grads).astype(bf16)
-    late_sum = lax.psum_scatter(late, "dp", scatter_dimension=0, tiled=True).astype(f32)
-    input_part, mixer_gain_grad = first_back(first_sum)
-    input_grad = middle_grad + input_part
-    own = jnp.concatenate(
-        [conv_grads[:4].reshape(-1), small[1, :DK], small[2, :DK]]
-    )
-    slots = jnp.zeros((tensor_size, own.shape[0]), f32)
-    slots = lax.dynamic_update_slice(slots, own[None, :], (tensor_index, 0))
-    everything = lax.psum(
-        jnp.concatenate([slots.reshape(-1), mixer_gain_grad, ffn_gain_grad, small[0]]),
-        ("dp", "tensor"),
-    )
-    own_sum = lax.dynamic_slice(
-        everything[: slots.size].reshape(slots.shape), (tensor_index, 0), (1, own.shape[0])
-    )[0]
-    gains = everything[slots.size :]
-    conv_sum = own_sum[: 4 * QKV].reshape(4, QKV)
+        mixed_grad, full, (proj, o, t, u, w, qe, a, s, tails), conv, dec, hg
+    )
+    pre_wgrad = contract_rows(first_rows, pre_grads)
+    weight_grads = jnp.concatenate(
+        [item.astype(bf16) for item in (pre_wgrad, out_wgrad, acts_wgrad, down_wgrad)], axis=1
+    )
+    gains = jnp.concatenate(
+        [jnp.zeros((1, D), f32), ffn_gain_grad, jnp.pad(small[0:1], ((0, 0), (0, D - DV))),
+         jnp.zeros((5, D), f32)],
+        axis=0,
+    )
+    heads = jnp.concatenate(
+        [conv_grads[:4], jnp.pad(small[1:3], ((0, 0), (0, QKV - DV))), jnp.zeros((2, QKV), f32)],
+        axis=0,
+    )
+    block_rows = D // DATA
+    vmem = pltpu.VMEM
+    input_grad, sums, gain_sums, head_sums = communicate(
+        end_kernel, 4,
+        [((local_rows, D), f32, False), ((block_rows, width), f32, False),
+         ((8, D), f32, False), ((8, QKV), f32, False)], False,
+        [scatter_slots, vmem((8, block_rows, width), bf16), vmem((8, block_rows, width), bf16),
+         vmem((8, block_rows, width), bf16), vmem((8, D), f32), vmem((TENSOR - 1, 8, D), f32),
+         vmem((8, D), f32), vmem((DATA - 1, 8, D), f32), vmem((DATA - 1, 8, QKV), f32)],
+        END_COPIES,
+        (first_part, weight_grads, block_input, middle_grad, mixer_gain[None, :], gains, heads),
+        "end_sums",
+    )
+    at = MIX
     return (
         block_output,
         input_grad,
-        gains[:D],
-        late_sum[:, :128],
-        late_sum[:, 128:256],
-        late_sum[:, 256:512],
-        late_sum[:, 512:768],
-        late_sum[:, 768:770].reshape(held, 1, 2),
-        conv_sum[:, :DK],
-        conv_sum[:, DK : 2 * DK],
-        conv_sum[:, 2 * DK :],
-        own_sum[4 * QKV : 4 * QKV + 1],
-        own_sum[4 * QKV + DK : 4 * QKV + DK + 1],
-        gains[2 * D :],
-        early_sum[:, 3 * ff :].T,
-        gains[D : 2 * D],
-        early_sum[:, :ff],
-        early_sum[:, ff : 2 * ff],
-        early_sum[:, 2 * ff : 3 * ff].T,
+        gain_sums[0],
+        sums[:, :128],
+        sums[:, 128:256],
+        sums[:, 256:512],
+        sums[:, 512:768],
+        sums[:, 768:770].reshape(depth, 1, 2),
+        head_sums[:4, :DK],
+        head_sums[:4, DK : 2 * DK],
+        head_sums[:4, 2 * DK :],
+        head_sums[4, :1],
+        head_sums[5, :1],
+        gain_sums[2, :DV],
+        sums[:, PRE:MIX].T,
+        gain_sums[1],
+        sums[:, at : at + ff],
+        sums[:, at + ff : at + 2 * ff],
+        sums[:, at + 2 * ff :].T,
     )
 
 

time: 863 us -> 418 us (0.48)
  waiting for transfers between devices: 703 us -> 0.04 us
  Pallas kernels: 52.7 us -> 316 us
  other arithmetic: 19.5 us -> 7.21 us
    pallas_call x1 -> x5, Pallas kernels: 26.2 us -> 289 us  [the longest x4 262 us: communicate(): pl.pallas_call(kernel, out_shape=[jax.ShapeDtypeStruct(shape, kind) for s...]
    reduce_scatter x4 -> x1, waiting for transfers between devices: 174 us -> 0.01 us  [row_sums(): lax.psum_scatter(values.astype(bf16), 'tensor', scatter_dimension=0, tile...]
    all_gather x4 -> x1, waiting for transfers between devices: 160 us -> 0.01 us  [group_rows(): return lax.all_gather(values, 'tensor', axis=0, tiled=True)]
    psum x1 -> x0, waiting for transfers between devices: 145 us -> none  [shards(): lax.psum(jnp.concatenate([slots.reshape(-1), mixer_gain_grad, ffn_gain_gr...]
    all_gather x2 -> x0, waiting for transfers between devices: 96.8 us -> none  [the longest x1 50.5 us: shards(): ffn_full = lax.all_gather(ffn_pack, 'dp', axis=0, tiled=True)]
    unnamed x14 -> x2, waiting for transfers between devices: 75.2 us -> 0.03 us
    reduce_scatter x1 -> x0, waiting for transfers between devices: 52.3 us -> none  [shards(): lax.psum_scatter(late, 'dp', scatter_dimension=0, tiled=True).astype(f32)]
    unnamed x73 -> x27, local copies, waits for them, and re-layouts: 14 us -> 2.1 us
  transfers between devices with their start and end apart: 13 -> 2, of which waited for: 13 -> 0; matrix products, arithmetic and copies ran while one was open for 6% -> 15% of each run, Pallas kernels for 0% -> 77%
where the time goes in v2:
time: 418 us; the launch traced here: 411 us
  Pallas kernels  316 us (76%)
  matrix products  40.7 us (10%)
  local copies, waits for them, and re-layouts  30.7 us (7%)
  between operations  16.7 us (4%)
  other arithmetic  7.21 us (2%)
    pallas_call x4, Pallas kernels, communicate(): pl.pallas_call(kernel, out_shape=[jax.ShapeDtypeStruct(shape, kind) for s...  262 us
    pallas_call x1, Pallas kernels, call_backward(): pl.pallas_call(mix_backward, grid=(steps,), in_specs=[tall(D), fixed((D,...  26.8 us
    pallas_call x1, Pallas kernels, call_forward(): pl.pallas_call(mix_forward, grid=(steps,), in_specs=[tall(D), fixed((D, M...  26.2 us
    dot_general x4, matrix products, contract_rows(): lax.dot_general(left_side, right_side, (((0,), (0,)), ((), ())), preferre...  15.6 us
    dot_general x2, matrix products, matmul(): return jnp.dot(left_side, right_side, preferred_element_type=f32)  13.7 us
    dot_general x2, matrix products, times_transposed(): lax.dot_general(left_side, right_side, (((1,), (1,)), ((), ())), preferre...  11.4 us
  transfers between devices with their start and end apart: 2, of which 0 were waited for; matrix products, arithmetic and copies ran while one was open for 15% of the time, Pallas kernels for 77%

profile of v2, /device:TPU:1, one launch (start us, length us, event | category | flops | bytes accessed | tf_op | source)
XLA Modules:
  0.0 410.9 jit_solution(13651115736902177753)
XLA Ops:
  7.2 0.0 all-gather.2.cloned.1.call-start
  7.9 0.0 copy-start.2
  7.9 0.6 copy-done.2
  8.5 1.9 multiply_convert_fusion.3
  10.3 0.0 all-gather.2.cloned.1.call-update
  10.4 0.0 reduce-scatter.2.cloned.1.call-start
  11.8 0.5 pad.31.clone
  12.3 0.6 pad.34.clone
  12.9 0.6 pad.30.clone
  13.4 0.8 copy.45
  14.2 0.7 fusion.6.live_ref
  14.9 0.1 fusion.11
  15.0 1.3 select_maximum_fusion.2.conv_ref
  16.3 1.8 concatenate.18.pack_ref
  18.0 65.5 %start_gathers.1 = (bf16[1536,1024]{1,0:T(8,128)(2,1)}, bf16[1024,2208]{1,0:T(8,128)(2,1)}) custom-call(bf16[192,1024]{1,0:T(8,128)(2,1)} %x_ref.5, f32[1,1024]{1,0:T(1,128)} %bitcast.39, bf16[64,2208]{1,0:T(8,128)(2,1)} %concatenate.18.pack_ref), custom_call_target="tpu_custom_call" | custom-call | flops 30000001024 | bytes 20000000 | tf_op jit(solution)/shard_map/start_gathers/pallas_call | solution.py:843
  83.6 0.7 pad.25.dec_ref
  84.2 26.2 %mix_forward.1 = (f32[1536,896]{1,0:T(8,128)}, bf16[1536,1024]{1,0:T(8,128)(2,1)}, bf16[1536,256]{1,0:T(8,128)(2,1)}, f32[1536,256]{1,0:T(8,128)}, bf16[6,256,25...) custom-call(bf16[1536,1024]{1,0:T(8,128)(2,1)} %get-tuple-element.45, ...), custom_call_target="tpu_custom_call" | custom-call | flops 30000001024 | bytes 20000000 | tf_op jit(solution)/shard_map/mix_forward/pallas_call | solution.py:339
  110.4 51.6 %middle_sums.1 = (f32[192,1024]{1,0:T(8,128)}, bf16[1536,1024]{1,0:T(8,128)(2,1)}) custom-call(bf16[1536,1024]{1,0:T(8,128)(2,1)} %get-tuple-element.47.part_ref, bf16[192,1024]{1,0:T(8,128)(2,1)} %x_ref.5, f32[192,1]{1,0:T(8,128)} %fusion.6.live_ref, f32[1,1024]{1,0:T(1,128)} %bitcast.37), custom_call_target="tpu_custom_call" | custom-call | flops 30000001024 | bytes 20000000 | tf_op jit(solution)/shard_map/middle_sums/pallas_call | solution.py:843
  162.0 6.9 %fusion.1 = f32[1536,704]{0,1:T(8,128)} fusion(bf16[1536,1024]{1,0:T(8,128)(2,1)} %get-tuple-element.49, bf16[1024,2208]{1,0:T(8,128)(2,1)} %get-tuple-element.46.pack_ref), kind=kOutput, calls=%fused_computation.10 | convolution fusion | flops 2214592512 | bytes 9043968 | tf_op jit(solution)/shard_map/dot_general | solution.py:862
  168.9 6.8 %multiply_convert_fusion.1 = (bf16[1536,352]{0,1:T(8,128)(2,1)S(1)}, bf16[1536,352]{0,1:T(8,128)(2,1)}, bf16[1536,352]{0,1:T(8,128)(2,1)S(1)}) fusion(f32[1536,704]{0,1:T(8,128)} %fusion.1, bf16[1536,1024]{1,0:T(8,128)(2,1)} %all-gather.2.cloned.1.call-done, bf16[1024,2208]{1,0:T(8,128)(2,1)} %get-tuple-element.46.pack_ref), kind=kOutput, calls=%fused_computation.4 | convolution fusion | flops 1115947008 | bytes 11501568 | tf_op jit(solution)/shard_map/dot_general | solution.py:862
  175.7 5.3 %convolution_convert_fusion.1 = bf16[1536,1024]{1,0:T(8,128)(2,1)} fusion(bf16[1536,352]{0,1:T(8,128)(2,1)S(1)} %get-tuple-element.73, bf16[1024,2208]{1,0:T(8,128)(2,1)} %get-tuple-element.46.pack_ref), kind=kOutput, calls=%fused_computation.1 | convolution fusion | flops 1108869120 | bytes 5013504 | tf_op jit(solution)/shard_map/dot_general | solution.py:872
  181.0 0.0 reduce-scatter.2.cloned.1.call-update
  181.0 0.0 copy-done.12
  181.0 6.2 %convolution_convert_fusion.part_ref = bf16[1536,1024]{1,0:T(8,128)(2,1)} fusion(bf16[1536,352]{0,1:T(8,128)(2,1)} %get-tuple-element.72, bf16[1536,352]{0,1:T(8,128)(2,1)S(1)} %get-tuple-element.71, bf16[1024,2208]{1,0:T(8,128)(2,1)} %get-tuple-element.46.pack_ref), kind=kOutput, calls=%fused_computation | convolution fusion | flops 2220490752 | bytes 6881280 | tf_op jit(solution)/shard_map/dot_general | solution.py:872
  187.2 79.5 %turn_sums.1 = (f32[192,1024]{1,0:T(8,128)}, bf16[1536,1024]{1,0:T(8,128)(2,1)}, f32[1,1024]{1,0:T(1,128)}) custom-call(bf16[1536,1024]{1,0:T(8,128)(2,1)} %convolution_convert_fusion.part_ref, f32[192,1024]{1,0:T(8,128)} %get-tuple-element.48.middle_ref, bf16[192,1024]{1,0:T(8,128)(2,1)} %cot_ref.1, f32[192,1]{1,0:T(8,128)} %fusion.6.live_ref, ...), custom_call_target="tpu_custom_call" | custom-call | flops 30000001024 | bytes 20000000 | tf_op jit(solution)/shard_map/turn_sums/pallas_call | solution.py:843
  266.7 0.0 copy-start.9
  266.7 26.8 %mix_backward.1 = (bf16[1536,896]{1,0:T(8,128)(2,1)}, bf16[1536,1024]{1,0:T(8,128)(2,1)}, f32[8,512]{1,0:T(8,128)}, f32[8,256]{1,0:T(8,128)}) custom-call(bf16[1536,1024]{1,0:T(8,128)(2,1)} %get-tuple-element.50.grad_ref, bf16[1024,2208]{1,0:T(8,128)(2,1)} %get-tuple-element.46.pack_ref, f32[1536,896]{1,0:T(8,128)} %get-tuple-element.51.proj_ref, ...), custom_call_target="tpu_custom_call" | custom-call | flops 60000002048 | bytes 20000000 | tf_op jit(solution)/shard_map/mix_backward/pallas_call | solution.py:378
  293.5 0.0 copy-done.9
  293.5 1.3 convolution_convert_fusion.4
  294.8 0.7 slice.76
  295.5 0.7 slice.78
  296.2 0.4 copy.49
  296.6 6.1 %convolution_convert_fusion.3 = bf16[1024,704]{0,1:T(8,128)(2,1)} fusion(bf16[1536,1024]{1,0:T(8,128)(2,1)} %get-tuple-element.49, bf16[1536,352]{0,1:T(8,128)(2,1)} %get-tuple-element.72, bf16[1536,352]{0,1:T(8,128)(2,1)} %copy-done.12), kind=kOutput, calls=%fused_computation.8 | convolution fusion | flops 2219638784 | bytes 6750208 | tf_op jit(solution)/shard_map/dot_general | solution.py:866
  302.7 1.7 copy.48
  304.4 0.0 copy-done.5
  304.5 0.0 copy-start.10
  304.5 0.0 copy-start.11
  304.5 3.3 convolution_convert_fusion.5
  307.7 0.0 copy-done.10
  307.8 0.6 copy-done.11
  308.4 4.9 %convolution_convert_fusion.2 = bf16[1024,896]{1,0:T(8,128)(2,1)} fusion(bf16[1536,1024]{1,0:T(8,128)(2,1)S(1)} %copy-done.10, bf16[1536,896]{1,0:T(8,128)(2,1)S(1)} %copy-done.11), kind=kOutput, calls=%fused_computation.7 | convolution fusion | flops 2819489792 | bytes 7733248 | tf_op jit(solution)/shard_map/dot_general | solution.py:866
  313.2 7.4 %concatenate.21.weight_ref = bf16[1024,2208]{1,0:T(8,128)(2,1)} concatenate(bf16[1024,896]{1,0:T(8,128)(2,1)} %convolution_convert_fusion.2, bf16[1024,256]{1,0:T(8,128)(2,1)S(1)} %convolution_convert_fusion.5, bf16[1024,704]{1,0:T(8,128)(2,1)S(1)} %copy.48, bf16[1024,352]{1,0:T(8,128)(2,1)S(1)} %copy.49), dimensions={1} | concatenate | bytes 9043968 | tf_op jit(solution)/shard_map/concatenate | solution.py:955
  320.7 0.0 copy-done.8
  320.7 0.7 fusion.9.head_ref
  321.3 0.0 copy-done.4
  321.3 0.0 copy-done.6
  321.4 0.0 copy-done.7
  321.4 0.7 fusion.7.gains_ref
  322.0 65.9 %end_sums.1 = (f32[192,1024]{1,0:T(8,128)}, f32[64,2208]{1,0:T(8,128)}, f32[8,1024]{1,0:T(8,128)}, f32[8,512]{1,0:T(8,128)}) custom-call(bf16[1536,1024]{1,0:T(8,128)(2,1)} %get-tuple-element.60.part_ref, bf16[1024,2208]{1,0:T(8,128)(2,1)} %concatenate.21.weight_ref, bf16[192,1024]{1,0:T(8,128)(2,1)} %x_ref.5, f32[192,1024]{1,0:T(8,128)} %get-tuple-element.63.grad_ref, ...), custom_call_target="tpu_custom_call" | custom-call | flops 30000001024 | bytes 20000000 | tf_op jit(solution)/shard_map/end_sums/pallas_call | solution.py:843
  388.0 0.0 copy-start
  388.0 1.3 slice.90
  389.3 1.3 slice.87
  390.6 0.8 slice.84
  391.4 0.6 copy.50
  392.0 1.3 fusion.16
  393.3 1.3 fusion.17
  394.6 1.4 fusion.15
  396.0 1.4 fusion.14
  397.4 1.6 slice_bitcast_fusion.1
  399.0 1.8 slice_bitcast_fusion
  400.8 0.0 copy-done.1
  400.8 0.0 copy-done.3
  400.8 1.9 add_convert_fusion
  402.7 0.9 copy.57
  (16 shorter events, 0.0 us)
Async XLA Ops:
  7.2 161.7 %all-gather.2.cloned.1.call-start = ((), (), s32[]{:S(2)}) async-start(), calls=%async_computation.2 | async-start | bytes 3538944 | tf_op jit(solution)/shard_map/all_gather | solution.py:878
  7.9 0.6 copy-start.2
  10.4 390.4 %reduce-scatter.2.cloned.1.call-start = ((), (), s32[]{:S(2)}) async-start(), calls=%async_computation.1 | async-start | bytes 3538944 | tf_op jit(solution)/shard_map/reduce_scatter | solution.py:882
  175.7 5.3 %copy-start.12 = (bf16[1536,352]{0,1:T(8,128)(2,1)}, bf16[1536,352]{0,1:T(8,128)(2,1)S(1)}, u32[]{:S(2)}) copy-start(bf16[1536,352]{0,1:T(8,128)(2,1)S(1)} %get-tuple-element.71) | copy-start | bytes 3244036
  266.7 26.9 %copy-start.9 = (bf16[1536,1024]{1,0:T(8,128)(2,1)S(1)}, bf16[1536,1024]{1,0:T(8,128)(2,1)}, u32[]{:S(2)}) copy-start(bf16[1536,1024]{1,0:T(8,128)(2,1)} %all-gather.2.cloned.1.call-done) | copy-start | bytes 9437188
  302.7 1.7 copy-start.5
  304.5 3.3 copy-start.10
  304.5 3.9 copy-start.11
  313.2 7.4 %copy-start.8 = (f32[8]{0:T(128)S(1)}, f32[8]{0:T(128)}, u32[]{:S(2)}) copy-start(f32[8]{0:T(128)} %pad.30.clone) | copy-start | bytes 100
  313.2 8.1 %copy-start.4 = (f32[1,1024]{1,0:T(1,128)S(1)}, f32[1,1024]{1,0:T(1,128)}, u32[]{:S(2)}) copy-start(f32[1,1024]{1,0:T(1,128)} %get-tuple-element.64) | copy-start | bytes 12292
  313.2 8.1 %copy-start.6 = (f32[8]{0:T(128)S(1)}, f32[8]{0:T(128)}, u32[]{:S(2)}) copy-start(f32[8]{0:T(128)} %pad.31.clone) | copy-start | bytes 100
  313.2 8.1 %copy-start.7 = (f32[8]{0:T(128)S(1)}, f32[8]{0:T(128)}, u32[]{:S(2)}) copy-start(f32[8]{0:T(128)} %pad.34.clone) | copy-start | bytes 100
  322.0 78.8 %copy-start.1 = (f32[192,1024]{1,0:T(8,128)S(1)}, f32[192,1024]{1,0:T(8,128)}, u32[]{:S(2)}) copy-start(f32[192,1024]{1,0:T(8,128)} %get-tuple-element.48.middle_ref) | copy-start | bytes 2359300
  322.0 78.8 %copy-start.3 = (f32[192]{0:T(256)S(1)}, f32[192]{0:T(256)}, u32[]{:S(2)}) copy-start(f32[192]{0:T(256)} %copy-done.2) | copy-start | bytes 2308
  388.0 14.7 %copy-start = (f32[192,1024]{1,0:T(8,128)S(1)}, f32[192,1024]{1,0:T(8,128)}, u32[]{:S(2)}) copy-start(f32[192,1024]{1,0:T(8,128)} %get-tuple-element.108) | copy-start | bytes 2359300
Sparse Core Ops, SparseCore 0:
  10.5 66.9 all-gather.1
  181.1 71.0 reduce-scatter.1
